TPU v7x, 256 devices: a whole 4x4x8 slice. The times are simulated.
256 devices in a mesh: dp: 4 (over z_hi), mx: 16 (over z_lo, y, core), my: 4 (over x).
Axes of the slice: x: 4, y: 4, z: 8 (z_hi: 4, z_lo: 2; z = z_hi * 2 + z_lo), core: 2. Of those that a mesh axis runs over, the one named last changes fastest.
Arguments:
- inputs: bfloat16 [1024, 6144], P(('dp', 'my'), 'mx'), may hold values from -18 to 18
- triple_weight: bfloat16 [6144, 3, 6144], P('mx', None, 'my'), may hold values from -0.078125 to 0.078125
- expand_weight: bfloat16 [6144, 12288], P('mx', 'my'), may hold values from -0.078125 to 0.078125
- merge_weight: bfloat16 [6144, 6144], P('mx', 'my'), may hold values from -0.078125 to 0.078125
- shrink_weight: bfloat16 [6144, 12288], P('mx', 'my'), may hold values from -0.0546875 to 0.0546875
- cotangent: bfloat16 [1024, 6144], P(('dp', 'my'), 'mx'), may hold values from -4 to 4
Outputs:
- outputs: bfloat16 [1024, 6144], P(('dp', 'my'), 'mx')
- block_input_gradient: bfloat16 [1024, 6144], P(('dp', 'my'), 'mx')
- triple_grad: bfloat16 [6144, 3, 6144], P(('mx', 'dp'), None, 'my')
- expand_grad: bfloat16 [6144, 12288], P(('mx', 'dp'), 'my')
- merge_grad: bfloat16 [6144, 6144], P(('mx', 'dp'), 'my')
- shrink_grad: bfloat16 [6144, 12288], P(('mx', 'dp'), 'my')
All inputs are finite; a program needn't handle non-finite values.
Results may differ from a plain program's by a relative error of at most 0.04.
Values may be sent and summed in bfloat16 or wider, within the bound.
A program may use at most 128 MiB of HBM per device.

v0:
```python
import math

import jax
import jax.numpy as jnp
from jax import lax
from jax.sharding import PartitionSpec as P

MODEL_WIDTH = 6144
HEAD_DIM = 128
PATCHES = 256


EPS = 1e-06
ROOT_HALF = 0.7071067811865476
INV_ROOT_TAU = 0.3989422804014327


def apply_layer_norm(block):
    centre = block - jnp.mean(block, axis=-1, keepdims=True)
    inverse = lax.rsqrt(jnp.mean(centre * centre, axis=-1, keepdims=True) + EPS)
    return (centre * inverse, inverse)


def layer_norm_backward(grad_in, unit, inverse):
    first_mean = jnp.mean(grad_in, axis=-1, keepdims=True)
    second_mean = jnp.mean(grad_in * unit, axis=-1, keepdims=True)
    return (grad_in - first_mean - unit * second_mean) * inverse


def gelu_slope(pre_act):
    return (
        0.5 * (1.0 + lax.erf(pre_act * ROOT_HALF))
        + pre_act * jnp.exp(-0.5 * pre_act * pre_act) * INV_ROOT_TAU
    )


def contract_last(left, right):
    return lax.dot_general(
        left, right, (((1,), (1,)), ((), ())), preferred_element_type=jnp.float32
    )


def contract_first(left, right):
    return lax.dot_general(
        left, right, (((0,), (0,)), ((), ())), preferred_element_type=jnp.float32
    )


def row_totals(pair):
    return lax.psum((pair[0], pair[1]), "mx")


def collect_row_blocks(block):
    return lax.all_gather(block, "my", axis=0, tiled=True)


def sum_rows(pair):
    return (
        lax.psum_scatter(
            pair[0].astype(jnp.bfloat16), "mx", scatter_dimension=0, tiled=True
        ).astype(jnp.float32),
        lax.psum_scatter(
            pair[1].astype(jnp.bfloat16), "mx", scatter_dimension=0, tiled=True
        ).astype(jnp.float32),
    )


def gather_share(pair):
    return (
        lax.all_gather(pair[0], "mx", axis=0, tiled=True),
        lax.all_gather(pair[1], "mx", axis=0, tiled=True),
    )


def key_totals(pair):
    return (
        lax.psum_scatter(
            pair[0].astype(jnp.bfloat16), "mx", scatter_dimension=0, tiled=True
        ).astype(jnp.float32),
        lax.psum_scatter(
            pair[1].astype(jnp.bfloat16), "mx", scatter_dimension=0, tiled=True
        ).astype(jnp.float32),
    )


def sum_features(term_fn, row_count):
    return lax.psum_scatter(
        term_fn(jnp.int32(0), row_count * lax.axis_size("my")).astype(jnp.bfloat16),
        "my",
        scatter_dimension=0,
        tiled=True,
    ).astype(jnp.float32)


def body(inputs, triple_weight, expand_weight, merge_weight, shrink_weight, cotangent):
    own_rows = inputs.shape[0]
    group_rows = own_rows * lax.axis_size("my")
    feat_here = inputs.shape[1]
    head_width = merge_weight.shape[1]
    heads_here = head_width // HEAD_DIM
    scale_factor = 1.0 / math.sqrt(HEAD_DIM)
    input_float_rows = inputs.astype(jnp.float32)
    row_total, row_square = row_totals(
        (jnp.sum(input_float_rows, axis=1), jnp.sum(input_float_rows * input_float_rows, axis=1))
    )
    mean_per_row = row_total / MODEL_WIDTH
    inverse_row_deviation = lax.rsqrt(row_square / MODEL_WIDTH - mean_per_row * mean_per_row + EPS)[
        :, None
    ]
    centered_scaled_input = (input_float_rows - mean_per_row[:, None]) * inverse_row_deviation
    normed_rows_full = collect_row_blocks(centered_scaled_input.astype(jnp.bfloat16))
    joined = triple_weight.reshape(feat_here, 3 * head_width)
    joined_term = jnp.dot(normed_rows_full, joined, preferred_element_type=jnp.float32)
    expand_term = jnp.dot(normed_rows_full, expand_weight, preferred_element_type=jnp.float32)
    projected, pre_act = sum_rows((joined_term, expand_term))
    first_row = lax.axis_index("mx") * projected.shape[0]
    row_count = projected.shape[0]
    qhat, q_inverse = apply_layer_norm(
        projected[:, :head_width].reshape(row_count, heads_here, HEAD_DIM)
    )
    khat, k_inverse = apply_layer_norm(
        projected[:, head_width : 2 * head_width].reshape(row_count, heads_here, HEAD_DIM)
    )
    q_half = qhat.astype(jnp.bfloat16)
    k_half = khat.astype(jnp.bfloat16).reshape(row_count, head_width)
    v_half = projected[:, 2 * head_width :].astype(jnp.bfloat16)
    keys_all, values_all = gather_share((k_half, v_half))
    keys_three = keys_all.reshape(group_rows, heads_here, HEAD_DIM)
    values_three = values_all.reshape(group_rows, heads_here, HEAD_DIM)
    query_image = (first_row + jnp.arange(row_count, dtype=jnp.int32)) // PATCHES
    key_image = jnp.arange(group_rows, dtype=jnp.int32) // PATCHES
    same_image = (query_image[:, None] == key_image[None, :])[None, :, :]
    scores = (
        jnp.einsum("qhd,khd->hqk", q_half, keys_three, preferred_element_type=jnp.float32)
        * scale_factor
    )
    expo = jnp.where(same_image, jnp.exp(scores), 0.0)
    probs = expo / jnp.sum(expo, axis=-1, keepdims=True)
    probs_half = probs.astype(jnp.bfloat16)
    attended = jnp.einsum(
        "hqk,khd->qhd", probs_half, values_three, preferred_element_type=jnp.float32
    )
    attended = attended.reshape(row_count, head_width).astype(jnp.bfloat16)
    hidden = jax.nn.gelu(pre_act, approximate=False).astype(jnp.bfloat16)
    attended_all, hidden_all = gather_share((attended, hidden))

    def forward_term(offset, length):
        return contract_last(attended_all, merge_weight) + contract_last(hidden_all, shrink_weight)

    branch = sum_features(forward_term, own_rows)
    outputs = (input_float_rows + branch).astype(jnp.bfloat16)
    upstream_all = collect_row_blocks(cotangent)
    att_term = jnp.dot(upstream_all, merge_weight, preferred_element_type=jnp.float32)
    hid_term = jnp.dot(upstream_all, shrink_weight, preferred_element_type=jnp.float32)
    d_attended, d_hidden = sum_rows((att_term, hid_term))
    d_att_half = d_attended.astype(jnp.bfloat16).reshape(row_count, heads_here, HEAD_DIM)
    d_probs = jnp.einsum(
        "qhd,khd->hqk", d_att_half, values_three, preferred_element_type=jnp.float32
    )
    d_scores = probs * (d_probs - jnp.sum(probs * d_probs, axis=-1, keepdims=True))
    d_scores_half = d_scores.astype(jnp.bfloat16)
    d_qn = (
        jnp.einsum("hqk,khd->qhd", d_scores_half, keys_three, preferred_element_type=jnp.float32)
        * scale_factor
    )
    d_kn = (
        jnp.einsum("hqk,qhd->khd", d_scores_half, q_half, preferred_element_type=jnp.float32)
        * scale_factor
    )
    d_values = jnp.einsum(
        "hqk,qhd->khd", probs_half, d_att_half, preferred_element_type=jnp.float32
    )
    d_kn_own, d_values_own = key_totals(
        (d_kn.reshape(group_rows, head_width), d_values.reshape(group_rows, head_width))
    )
    d_query = layer_norm_backward(d_qn, qhat, q_inverse).reshape(row_count, head_width)
    d_key = layer_norm_backward(
        d_kn_own.reshape(row_count, heads_here, HEAD_DIM), khat, k_inverse
    ).reshape(row_count, head_width)
    d_joined = jnp.concatenate([d_query, d_key, d_values_own], axis=1).astype(jnp.bfloat16)
    d_pre = (d_hidden * gelu_slope(pre_act)).astype(jnp.bfloat16)
    d_joined_all, d_pre_all = gather_share((d_joined, d_pre))

    def backward_term(offset, length):
        return contract_last(d_joined_all, joined) + contract_last(d_pre_all, expand_weight)

    grad_normalized_rows = sum_features(backward_term, own_rows)
    combined_gradient, cross_gradient = row_totals(
        (
            jnp.sum(grad_normalized_rows, axis=1),
            jnp.sum(grad_normalized_rows * centered_scaled_input, axis=1),
        )
    )
    correction = (
        grad_normalized_rows
        - combined_gradient[:, None] / MODEL_WIDTH
        - centered_scaled_input * (cross_gradient[:, None] / MODEL_WIDTH)
    ) * inverse_row_deviation
    block_input_gradient = (cotangent.astype(jnp.float32) + correction).astype(jnp.bfloat16)
    joined_part = contract_first(normed_rows_full, d_joined_all)
    expand_part = contract_first(normed_rows_full, d_pre_all)
    merge_part = contract_first(upstream_all, attended_all)
    shrink_part = contract_first(upstream_all, hidden_all)
    joined_sum, expand_sum, merge_sum, shrink_sum = (
        lax.psum_scatter(
            joined_part.astype(jnp.bfloat16), "dp", scatter_dimension=0, tiled=True
        ).astype(jnp.float32),
        lax.psum_scatter(
            expand_part.astype(jnp.bfloat16), "dp", scatter_dimension=0, tiled=True
        ).astype(jnp.float32),
        lax.psum_scatter(
            merge_part.astype(jnp.bfloat16), "dp", scatter_dimension=0, tiled=True
        ).astype(jnp.float32),
        lax.psum_scatter(
            shrink_part.astype(jnp.bfloat16), "dp", scatter_dimension=0, tiled=True
        ).astype(jnp.float32),
    )
    triple_grad = joined_sum.astype(jnp.bfloat16).reshape(joined_sum.shape[0], 3, head_width)
    return (
        outputs,
        block_input_gradient,
        triple_grad,
        expand_sum.astype(jnp.bfloat16),
        merge_sum.astype(jnp.bfloat16),
        shrink_sum.astype(jnp.bfloat16),
    )


def solution(mesh):
    placed = (
        P(("dp", "my"), "mx"),
        P("mx", None, "my"),
        P("mx", "my"),
        P("mx", "my"),
        P("mx", "my"),
        P(("dp", "my"), "mx"),
    )
    return jax.shard_map(
        body,
        mesh=mesh,
        in_specs=placed,
        out_specs=(
            P(("dp", "my"), "mx"),
            P(("dp", "my"), "mx"),
            P(("mx", "dp"), None, "my"),
            P(("mx", "dp"), "my"),
            P(("mx", "dp"), "my"),
            P(("mx", "dp"), "my"),
        ),
        check_vma=False,
    )
```

profile of v0, /device:TPU:1, one launch (start us, length us, event | category | flops | bytes accessed | tf_op | source)
XLA Modules:
  0.0 862.7 jit_solution(1493504931471038251)
XLA Ops:
  8.3 29.7 %all-reduce.1 = (f32[64]{0:T(128)S(1)}, f32[64]{0:T(128)S(1)}) all-reduce(f32[64]{0:T(128)S(1)} %get-tuple-element.37, f32[64]{0:T(128)S(1)} %get-tuple-element.36), channel_id=1, replica_groups=mesh['dp'=4,'mx'=16,'my'=4] {'mx'}, use_global_device_ids=true, to_apply=%region_3.0 | all-reduce | flops 128 | bytes 1024 | tf_op jit(solution)/shard_map/psum | solution.py:50
  39.5 9.2 %all_gather.24 = bf16[256,384]{1,0:T(8,128)(2,1)S(1)} all-gather(bf16[64,384]{1,0:T(8,128)(2,1)S(1)} %fusion.54), channel_id=1, replica_groups=mesh['dp'=4,'mx'=16,'my'=4] {'my'}, dimensions={0}, use_global_device_ids=true | all-gather | bytes 245760 | tf_op jit(solution)/shard_map/all_gather | solution.py:54
  48.7 6.0 copy.71
  54.8 4.9 convolution_convert_fusion.1
  60.4 9.2 %all_gather.29 = bf16[256,384]{1,0:T(8,128)(2,1)S(1)} all-gather(bf16[64,384]{1,0:T(8,128)(2,1)S(1)} %copy-done.8), channel_id=1, replica_groups=mesh['dp'=4,'mx'=16,'my'=4] {'my'}, dimensions={0}, use_global_device_ids=true | all-gather | bytes 245760 | tf_op jit(solution)/shard_map/all_gather | solution.py:54
  69.7 2.7 convolution_convert_fusion.7
  73.2 53.8 %reduce-scatter.17.cloned.1.call-done = bf16[16,4608]{1,0:T(8,128)(2,1)} async-done(((bf16[256,4608]{1,0:T(8,128)(2,1)}), bf16[16,4608]{1,0:T(8,128)(2,1)}) %reduce-scatter.17.cloned.1.call-update) | async-done | bytes 147472 | tf_op jit(solution)/shard_map/reduce_scatter | solution.py:59
  131.3 22.8 %all_gather.26 = bf16[256,1536]{1,0:T(8,128)(2,1)S(1)} all-gather(bf16[16,1536]{1,0:T(8,128)(2,1)} %get-tuple-element.43), channel_id=1, replica_groups=mesh['dp'=4,'mx'=16,'my'=4] {'mx'}, dimensions={0}, use_global_device_ids=true | all-gather | bytes 835584 | tf_op jit(solution)/shard_map/all_gather | solution.py:70
  156.1 21.5 %all_gather.25 = bf16[256,1536]{1,0:T(8,128)(2,1)} all-gather(bf16[16,1536]{1,0:T(8,128)(2,1)S(1)} %slice.13), channel_id=1, replica_groups=mesh['dp'=4,'mx'=16,'my'=4] {'mx'}, dimensions={0}, use_global_device_ids=true | all-gather | bytes 835584 | tf_op jit(solution)/shard_map/all_gather | solution.py:71
  179.0 13.4 %reduce-scatter.23.cloned.1.call-done = bf16[16,1536]{1,0:T(8,128)(2,1)} async-done(((bf16[256,1536]{1,0:T(8,128)(2,1)}), bf16[16,1536]{1,0:T(8,128)(2,1)}) %reduce-scatter.23.cloned.1.call-update) | async-done | bytes 49168 | tf_op jit(solution)/shard_map/reduce_scatter | solution.py:59
  192.4 1.7 fusion.66
  194.1 2.9 multiply_reduce_fusion
  198.7 2.4 multiply_convert_fusion
  201.0 2.3 copy.89
  203.4 2.3 convolution_convert_fusion.8
  205.7 2.3 copy.91
  208.0 2.2 convolution_convert_fusion.5
  210.3 3.9 convolution_convert_fusion.4
  214.2 2.8 fusion.76
  225.1 1.7 copy_bitcast_fusion.1
  226.8 38.1 %reduce-scatter.25.cloned.1.call-done = bf16[16,1536]{1,0:T(8,128)(2,1)} async-done(((bf16[256,1536]{1,0:T(8,128)(2,1)}), bf16[16,1536]{1,0:T(8,128)(2,1)}) %reduce-scatter.25.cloned.1.call-update) | async-done | bytes 49168 | tf_op jit(solution)/shard_map/reduce_scatter | solution.py:77
  267.8 1.8 fusion.59
  269.6 59.3 %reduce-scatter.27.cloned.1.call-done = bf16[16,1536]{1,0:T(8,128)(2,1)} async-done(((bf16[256,1536]{1,0:T(8,128)(2,1)}), bf16[16,1536]{1,0:T(8,128)(2,1)}) %reduce-scatter.27.cloned.1.call-update) | async-done | bytes 49168 | tf_op jit(solution)/shard_map/reduce_scatter | solution.py:80
  328.9 1.5 pad_maximum_fusion
  330.4 63.9 %reduce-scatter.19.cloned.1.call-done = bf16[16,3072]{1,0:T(8,128)(2,1)} async-done(((bf16[256,3072]{1,0:T(8,128)(2,1)}), bf16[16,3072]{1,0:T(8,128)(2,1)}) %reduce-scatter.19.cloned.1.call-update) | async-done | bytes 98320 | tf_op jit(solution)/shard_map/reduce_scatter | solution.py:62
  394.3 65.4 %reduce-scatter.29.cloned.1.call-done = bf16[16,3072]{1,0:T(8,128)(2,1)} async-done(((bf16[256,3072]{1,0:T(8,128)(2,1)}), bf16[16,3072]{1,0:T(8,128)(2,1)}) %reduce-scatter.29.cloned.1.call-update) | async-done | bytes 98320 | tf_op jit(solution)/shard_map/reduce_scatter | solution.py:62
  459.7 2.1 fusion.46
  463.8 23.2 %all_gather.27 = bf16[256,1536]{1,0:T(8,128)(2,1)S(1)} all-gather(bf16[16,1536]{1,0:T(8,128)(2,1)S(1)} %bitcast.142), channel_id=1, replica_groups=mesh['dp'=4,'mx'=16,'my'=4] {'mx'}, dimensions={0}, use_global_device_ids=true | all-gather | bytes 835584 | tf_op jit(solution)/shard_map/all_gather | solution.py:70
  487.1 14.6 %all-gather.6.cloned.1.call-done = bf16[256,4608]{1,0:T(8,128)(2,1)} async-done(((bf16[16,4608]{1,0:T(8,128)(2,1)}), bf16[256,4608]{1,0:T(8,128)(2,1)}) %all-gather.6.cloned.1.call-update) | async-done | bytes 2359312 | tf_op jit(solution)/shard_map/all_gather | solution.py:70
  501.7 4.9 fusion.81
  506.5 33.6 %all-gather.8.cloned.1.call-done = bf16[256,3072]{1,0:T(8,128)(2,1)} async-done(((bf16[16,3072]{1,0:T(8,128)(2,1)}), bf16[256,3072]{1,0:T(8,128)(2,1)}) %all-gather.8.cloned.1.call-update) | async-done | bytes 1572880 | tf_op jit(solution)/shard_map/all_gather | solution.py:71
  540.1 3.2 fusion.3
  543.5 2.6 fusion.80
  546.1 31.8 %all-gather.4.cloned.1.call-done = bf16[256,3072]{1,0:T(8,128)(2,1)} async-done(((bf16[16,3072]{1,0:T(8,128)(2,1)}), bf16[256,3072]{1,0:T(8,128)(2,1)}) %all-gather.4.cloned.1.call-update) | async-done | bytes 1572880 | tf_op jit(solution)/shard_map/all_gather | solution.py:71
  577.9 3.9 fusion.2
  581.9 4.5 convolution_convert_fusion
  586.5 1.6 fusion.1
  588.1 2.4 copy.99
  590.6 3.6 convolution_convert_fusion.3
  594.3 3.9 fusion
  598.2 4.3 copy.101
  604.3 27.6 %all-reduce = (f32[64]{0:T(128)S(1)}, f32[64]{0:T(128)S(1)}) all-reduce(f32[64]{0:T(128)S(1)} %get-tuple-element.35, f32[64]{0:T(128)S(1)} %get-tuple-element.34), channel_id=1, replica_groups=mesh['dp'=4,'mx'=16,'my'=4] {'mx'}, use_global_device_ids=true, to_apply=%region_25.26 | all-reduce | flops 128 | bytes 1024 | tf_op jit(solution)/shard_map/psum | solution.py:50
  631.9 1.6 fusion.50
  633.5 72.0 %reduce-scatter.33.cloned.1.call-done = bf16[96,4608]{1,0:T(8,128)(2,1)} async-done(((bf16[384,4608]{1,0:T(8,128)(2,1)}), bf16[96,4608]{1,0:T(8,128)(2,1)}) %reduce-scatter.33.cloned.1.call-update) | async-done | bytes 884752 | tf_op jit(solution)/shard_map/reduce_scatter | solution.py:205
  705.4 2.2 copy.154
  707.6 35.6 %reduce-scatter.37.cloned.1.call-done = bf16[96,1536]{1,0:T(8,128)(2,1)} async-done(((bf16[384,1536]{1,0:T(8,128)(2,1)}), bf16[96,1536]{1,0:T(8,128)(2,1)}) %reduce-scatter.37.cloned.1.call-update) | async-done | bytes 294928
  743.2 56.7 %reduce-scatter.35.cloned.1.call-done = bf16[96,3072]{1,0:T(8,128)(2,1)} async-done(((bf16[384,3072]{1,0:T(8,128)(2,1)}), bf16[96,3072]{1,0:T(8,128)(2,1)}) %reduce-scatter.35.cloned.1.call-update) | async-done | bytes 589840 | tf_op jit(solution)/shard_map/reduce_scatter | solution.py:208
  799.9 56.2 %reduce-scatter.39.cloned.1.call-done = bf16[96,3072]{1,0:T(8,128)(2,1)} async-done(((bf16[384,3072]{1,0:T(8,128)(2,1)}), bf16[96,3072]{1,0:T(8,128)(2,1)}) %reduce-scatter.39.cloned.1.call-update) | async-done | bytes 589840
  (108 shorter events, 28.9 us)
Async XLA Ops:
  7.2 200.9 %copy-start = (bf16[384,3072]{1,0:T(8,128)(2,1)S(1)}, bf16[384,3072]{1,0:T(8,128)(2,1)}, u32[]{:S(2)}) copy-start(bf16[384,3072]{1,0:T(8,128)(2,1)} %param.8) | copy-start | bytes 7077892
  7.2 119.8 %reduce-scatter.17.cloned.1.call-start = ((), (), s32[]{:S(2)}) async-start(), calls=%async_computation.12 | async-start | bytes 2506752 | tf_op jit(solution)/shard_map/reduce_scatter | solution.py:59
  38.0 0.5 copy-start.12
  38.0 1.4 copy-start.14
  59.6 0.8 copy-start.8
  59.7 132.7 %reduce-scatter.23.cloned.1.call-start = ((), (), s32[]{:S(2)}) async-start(), calls=%async_computation.16 | async-start | bytes 835584 | tf_op jit(solution)/shard_map/reduce_scatter | solution.py:59
  72.4 192.5 %reduce-scatter.25.cloned.1.call-start = ((), (), s32[]{:S(2)}) async-start(), calls=%async_computation.17 | async-start | bytes 835584 | tf_op jit(solution)/shard_map/reduce_scatter | solution.py:77
  127.8 3.4 copy-start.2
  127.9 3.3 copy-start.10
  129.3 1.9 copy-start.5
  129.3 1.9 copy-start.11
  129.5 1.8 copy-start.3
  129.6 1.7 copy-start.4
  130.3 0.6 copy-start.1
  198.0 0.6 copy-start.6
  203.3 125.5 %reduce-scatter.27.cloned.1.call-start = ((), (), s32[]{:S(2)}) async-start(), calls=%async_computation.18 | async-start | bytes 835584 | tf_op jit(solution)/shard_map/reduce_scatter | solution.py:80
  208.0 186.3 %reduce-scatter.19.cloned.1.call-start = ((), (), s32[]{:S(2)}) async-start(), calls=%async_computation.13 | async-start | bytes 1671168 | tf_op jit(solution)/shard_map/reduce_scatter | solution.py:62
  210.2 249.5 %reduce-scatter.29.cloned.1.call-start = ((), (), s32[]{:S(2)}) async-start(), calls=%async_computation.20 | async-start | bytes 1671168 | tf_op jit(solution)/shard_map/reduce_scatter | solution.py:62
  214.2 287.5 %all-gather.6.cloned.1.call-start = ((), (), s32[]{:S(2)}) async-start(), calls=%async_computation.19 | async-start | bytes 2506752 | tf_op jit(solution)/shard_map/all_gather | solution.py:70
  330.4 209.7 %all-gather.8.cloned.1.call-start = ((), (), s32[]{:S(2)}) async-start(), calls=%async_computation.21 | async-start | bytes 1671168 | tf_op jit(solution)/shard_map/all_gather | solution.py:71
  461.8 116.1 %all-gather.4.cloned.1.call-start = ((), (), s32[]{:S(2)}) async-start(), calls=%async_computation.14 | async-start | bytes 1671168 | tf_op jit(solution)/shard_map/all_gather | solution.py:71
  462.5 140.0 %reduce-scatter.31.cloned.1.call-start = ((), (), s32[]{:S(2)}) async-start(), calls=%async_computation.22 | async-start | bytes 245760 | tf_op jit(solution)/shard_map/reduce_scatter | solution.py:87
  543.3 88.6 %reduce-scatter.21.cloned.1.call-start = ((), (), s32[]{:S(2)}) async-start(), calls=%async_computation.15 | async-start | bytes 245760 | tf_op jit(solution)/shard_map/reduce_scatter | solution.py:87
  581.8 123.6 %reduce-scatter.33.cloned.1.call-start = ((), (), s32[]{:S(2)}) async-start(), calls=%async_computation.23 | async-start | bytes 4423680 | tf_op jit(solution)/shard_map/reduce_scatter | solution.py:205
  586.4 156.8 %reduce-scatter.37.cloned.1.call-start = ((), (), s32[]{:S(2)}) async-start(), calls=%async_computation.25 | async-start | bytes 1474560
  590.5 209.4 %reduce-scatter.35.cloned.1.call-start = ((), (), s32[]{:S(2)}) async-start(), calls=%async_computation.24 | async-start | bytes 2949120 | tf_op jit(solution)/shard_map/reduce_scatter | solution.py:208
  594.3 261.9 %reduce-scatter.39.cloned.1.call-start = ((), (), s32[]{:S(2)}) async-start(), calls=%async_computation.26 | async-start | bytes 2949120
  602.5 0.8 copy-start.7
  602.5 0.8 copy-start.13
  602.5 0.8 copy-start.15
  602.5 29.4 %copy-start.9 = (bf16[64,384]{1,0:T(8,128)(2,1)S(1)}, bf16[64,384]{1,0:T(8,128)(2,1)}, u32[]{:S(2)}) copy-start(bf16[64,384]{1,0:T(8,128)(2,1)} %param.11) | copy-start | bytes 147460
Sparse Core Ops, SparseCore 0:
  59.8 67.1 reduce-scatter.16
  130.0 62.2 reduce-scatter.22
  203.5 61.3 reduce-scatter.24
  267.2 61.5 reduce-scatter.26
  331.4 62.8 reduce-scatter.18
  396.7 62.9 reduce-scatter.28
  462.2 39.3 all-gather.5
  504.2 35.8 all-gather.7
  542.1 35.7 all-gather.3
  581.0 20.4 reduce-scatter.30
  604.0 22.9 reduce-scatter.20
  629.6 75.7 reduce-scatter.32
  708.8 34.4 reduce-scatter.36
  746.4 53.5 reduce-scatter.34
  803.1 53.0 reduce-scatter.38
where the time goes:
time: 865 us; the launch traced here: 863 us
  waiting for transfers between devices  595 us (69%)
  blocking collectives  143 us (17%)
  matrix products  55 us (6%)
  local copies, waits for them, and re-layouts  34.6 us (4%)
  other arithmetic  19.5 us (2%)
  between operations  14.3 us (2%)
    reduce_scatter x2, waiting for transfers between devices, sum_rows(): lax.psum_scatter(pair[1].astype(jnp.bfloat16), 'mx', scatter_dimension=0,...  129 us
    unnamed x17, waiting for transfers between devices  92.7 us
    reduce_scatter x1, waiting for transfers between devices, body(): lax.psum_scatter(joined_part.astype(jnp.bfloat16), 'dp', scatter_dimensio...  72 us
    reduce_scatter x2, waiting for transfers between devices, sum_rows(): lax.psum_scatter(pair[0].astype(jnp.bfloat16), 'mx', scatter_dimension=0,...  67.2 us
    all_gather x2, waiting for transfers between devices, gather_share(): lax.all_gather(pair[1], 'mx', axis=0, tiled=True)  65.4 us
    reduce_scatter x1, waiting for transfers between devices, key_totals(): lax.psum_scatter(pair[1].astype(jnp.bfloat16), 'mx', scatter_dimension=0,...  59.3 us
    psum x2, blocking collectives, row_totals(): return lax.psum((pair[0], pair[1]), 'mx')  57.3 us
    reduce_scatter x1, waiting for transfers between devices, body(): lax.psum_scatter(expand_part.astype(jnp.bfloat16), 'dp', scatter_dimensio...  56.7 us
  transfers between devices with their start and end apart: 15, of which 13 were waited for; matrix products, arithmetic and copies ran while one was open for 10% of the time, Pallas kernels for 0%

commit v1 on v0

v1 whole, which is shorter than its diff:
```python
import functools
import math

import jax
import jax.numpy as jnp
from jax import lax
from jax.experimental import pallas as pl
from jax.experimental.pallas import tpu as pltpu
from jax.sharding import PartitionSpec as P

MESH = pl.DeviceIdType.MESH
F32 = jnp.float32
BF16 = jnp.bfloat16

WIDTH = 6144
EPS = 1e-06
ROOT_HALF = 0.7071067811865476
INV_ROOT_TAU = 0.3989422804014327
SCALE = 1.0 / math.sqrt(128)
VMEM_LIMIT = 56 * 1024 * 1024

SEQ = ((0, 1, 2), (1, 2, 0), (2, 0, 1))


def place():
    m = lax.axis_index("mx")
    c = m % 2
    y = (m // 2) % 4
    z = m // 8
    return lax.axis_index("dp"), m, lax.axis_index("my"), y, z, c


def partners(m, y, z, c):
    return (m + 2 * (1 - 2 * (y % 2)), m + 2 * (3 - 2 * y), m + 8 - 16 * z, m + 1 - 2 * c)


def owner_of(y, z, c, da, db, dz, dc):
    b = (y // 2 + db) % 2
    a = (y + y // 2 + da) % 2
    return 2 * b + (a + b) % 2, (z + dz) % 2, (c + dc) % 2


def slot_bits(p, t):
    d = (t // 4, (t // 2) % 2, t % 2)
    bits = [None, None, None]
    for place_at, axis in enumerate(SEQ[p]):
        bits[axis] = d[place_at]
    return bits


def share_columns(yo, zo, co):
    k = zo * 2 + co
    head = 3 * yo + k
    unit = 6 * yo + k
    usual = (("m", head), ("s", unit), ("t", head), ("t", 12 + head), ("t", 24 + head), ("e", unit))
    first = 6 * yo + 3
    fourth = (("s", first), ("s", first + 1), ("s", first + 2), ("e", first), ("e", first + 1), ("e", first + 2))
    return k == 3, usual, fourth


def lanes(index):
    return pl.ds(pl.multiple_of(index * 128, 128), 128)


def load_weights(p, refs, held, sem, y, z, c):
    def step(s, carry):
        yo, zo, co = owner_of(y, z, c, s // 8, (s // 4) % 2, (s // 2) % 2, s % 2)
        fourth, usual, last = share_columns(yo, zo, co)

        def start(blocks):
            for half in range(2):
                name, index = blocks[2 * p + half]
                pltpu.make_async_copy(
                    refs[name].at[:, lanes(index)], held.at[p, s, :, pl.ds(128 * half, 128)], sem.at[p]
                ).start()

        @pl.when(fourth)
        def _():
            start(last)

        @pl.when(jnp.logical_not(fourth))
        def _():
            start(usual)

        return carry

    lax.fori_loop(0, 16, step, 0)


def wait_weights(p, held, sem):
    pltpu.make_async_copy(held.at[p], held.at[p], sem.at[p]).wait()


def remote(src, dst, send, recv, device):
    return pltpu.make_async_remote_copy(
        src_ref=src, dst_ref=dst, send_sem=send, recv_sem=recv, device_id=device, device_id_type=MESH
    )


def greet(devices):
    barrier = pltpu.get_barrier_semaphore()
    for device in devices:
        pl.semaphore_signal(barrier, inc=1, device_id=device, device_id_type=MESH)
    pl.semaphore_wait(barrier, len(devices))


def dot_last(left, right):
    return lax.dot_general(left, right, (((1,), (1,)), ((), ())), preferred_element_type=F32)


def dot_first(left, right):
    return lax.dot_general(left, right, (((0,), (0,)), ((), ())), preferred_element_type=F32)


def project_kernel(
    inp, cot, tri, exp, mer, shr, out, nown, nfull, cfull, unit_out, inv_out,
    held, part, got0, got1, got2, got3, stat_out, stat_in, both,
    wsem, xs, xr, ss, sr, rs, rr,
):
    r, m, x, y, z, c = place()
    refs = {"t": tri, "e": exp, "m": mer, "s": shr}
    peers = partners(m, y, z, c)
    xpeers = [(x + i) % 4 for i in (1, 2, 3)]
    load_weights(0, refs, held, wsem, y, z, c)
    greet([{"my": q} for q in xpeers] + [{"mx": q} for q in peers])

    own = pl.ds(pl.multiple_of(x * 64, 64), 64)
    sends = []
    for i in range(3):
        copy = remote(cot, cfull.at[own], xs.at[0, i], xr.at[0, i], {"my": xpeers[i]})
        copy.start()
        sends.append(copy)
    cfull[own, :] = cot[...]

    rows = inp[...].astype(F32)
    mean = jnp.sum(rows, axis=1, keepdims=True) / rows.shape[1]
    centred = rows - mean
    square = jnp.sum(centred * centred, axis=1, keepdims=True)
    low = lax.broadcasted_iota(jnp.int32, (64, 128), 1) < 64
    count = float(rows.shape[1])
    for step in range(4):
        stat_out[step] = jnp.where(low, mean, square)
        copy = remote(
            stat_out.at[step], stat_in.at[step], ss.at[step], sr.at[step], {"mx": peers[(3, 0, 1, 2)[step]]}
        )
        copy.start()
        if step == 0:
            for p in (1, 2):
                load_weights(p, refs, held, wsem, y, z, c)
        copy.wait_recv()
        sends.append(copy)
        other = stat_in[step]
        mean2, square2 = other[:, 0:1], other[:, 64:65]
        delta = mean2 - mean
        square = square + square2 + delta * delta * (count / 2)
        mean = (mean + mean2) * 0.5
        count = count * 2
    inverse = lax.rsqrt(square / WIDTH + EPS)
    unit = (rows - mean) * inverse
    unit_out[...] = unit
    inv_out[...] = jnp.broadcast_to(inverse, (64, 128))
    nown[...] = unit.astype(BF16)
    nfull[own, :] = unit.astype(BF16)
    for i in range(3):
        copy = remote(nown, nfull.at[own], xs.at[1, i], xr.at[1, i], {"my": xpeers[i]})
        copy.start()
        sends.append(copy)

    def gathered(k, full):
        for i in range(3):
            rows_of = pl.ds(pl.multiple_of(((x + 3 - i) % 4) * 64, 64), 64)
            remote(full.at[rows_of], full.at[rows_of], xs.at[k, i], xr.at[k, i], {"my": xpeers[i]}).wait_recv()

    def multiply(p, dc):
        def step(t, carry):
            da, db, dz = slot_bits(p, t)
            s = da * 8 + db * 4 + dz * 2 + dc
            if p == 1:
                fourth = ((z + dz) % 2) * ((c + dc) % 2)
                first = jnp.dot(both[fourth], held[p, s, :, 0:128], preferred_element_type=F32)
                second = jnp.dot(both[0], held[p, s, :, 128:256], preferred_element_type=F32)
                part[p, dc, t, :, 0:128] = first.astype(BF16)
                part[p, dc, t, :, 128:256] = second.astype(BF16)
            else:
                full = both[1 if p == 0 else 0]
                part[p, dc, t] = jnp.dot(full, held[p, s], preferred_element_type=F32).astype(BF16)
            return carry

        lax.fori_loop(0, 8, step, 0)

    def stage(p, k):
        if k == 0:
            return remote(part.at[p, 1], got0.at[p], rs.at[p, 0], rr.at[p, 0], {"mx": peers[3]})
        size = 8 >> k
        target = (None, got1, got2, got3)[k]
        return remote(
            part.at[p, 0, pl.ds(size, size)], target.at[p], rs.at[p, k], rr.at[p, k],
            {"mx": peers[SEQ[p][k - 1]]},
        )

    def absorb(p, k):
        stage(p, k).wait_recv()
        source = (got0, got1, got2, got3)[k]

        def step(t, carry):
            part[p, 0, t] = (part[p, 0, t].astype(F32) + source[p, t].astype(F32)).astype(BF16)
            return carry

        if k < 3:
            lax.fori_loop(0, 8 >> k, step, 0)
        else:
            out[p] = part[p, 0, 0].astype(F32) + source[p, 0].astype(F32)

    gathered(0, cfull)
    both[1] = cfull[...]
    wait_weights(0, held, wsem)
    multiply(0, 1)
    stage(0, 0).start()
    multiply(0, 0)
    gathered(1, nfull)
    both[0] = nfull[...]
    wait_weights(1, held, wsem)
    multiply(1, 1)
    stage(1, 0).start()
    multiply(1, 0)
    absorb(0, 0)
    stage(0, 1).start()
    wait_weights(2, held, wsem)
    multiply(2, 1)
    stage(2, 0).start()
    multiply(2, 0)
    absorb(1, 0)
    stage(1, 1).start()
    absorb(2, 0)
    stage(2, 1).start()
    for k in (1, 2):
        for p in range(3):
            absorb(p, k)
            stage(p, k + 1).start()
    for p in range(3):
        absorb(p, 3)
    for copy in sends:
        copy.wait_send()
    for p in range(3):
        for k in range(4):
            stage(p, k).wait_send()


def norm_heads(block):
    centre = block - jnp.mean(block, axis=-1, keepdims=True)
    inverse = lax.rsqrt(jnp.mean(centre * centre, axis=-1, keepdims=True) + EPS)
    return centre * inverse, inverse


def norm_backward(grad, unit, inverse):
    first = jnp.mean(grad, axis=-1, keepdims=True)
    second = jnp.mean(grad * unit, axis=-1, keepdims=True)
    return (grad - first - unit * second) * inverse


def gelu_pair(pre):
    phi = 0.5 * (1.0 + lax.erf(pre * ROOT_HALF))
    return pre * phi, phi + pre * jnp.exp(-0.5 * pre * pre) * INV_ROOT_TAU


def middle_kernel(proj, out):
    r, m, x, y, z, c = place()
    fourth = z * 2 + c == 3

    def left(p):
        return (p, slice(None), slice(0, 128))

    def right(p):
        return (p, slice(None), slice(128, 256))

    def unit(pre_at, grad_at):
        value, slope = gelu_pair(proj[pre_at])
        grad = proj[grad_at]
        out[grad_at] = value.astype(BF16)
        out[pre_at] = (grad * slope).astype(BF16)

    @pl.when(fourth)
    def _():
        unit(right(1), left(0))
        unit(left(2), right(0))
        unit(right(2), left(1))

    @pl.when(jnp.logical_not(fourth))
    def _():
        unit(right(2), right(0))
        qhat, qinv = norm_heads(proj[left(1)])
        khat, kinv = norm_heads(proj[right(1)])
        q, k = qhat.astype(BF16), khat.astype(BF16)
        v = proj[left(2)].astype(BF16)
        datt = proj[left(0)].astype(BF16)
        expo = jnp.exp(dot_last(q, k) * SCALE)
        probs = expo / jnp.sum(expo, axis=-1, keepdims=True)
        half = probs.astype(BF16)
        out[left(0)] = jnp.dot(half, v, preferred_element_type=F32).astype(BF16)
        g = dot_last(datt, v)
        ds = (probs * (g - jnp.sum(probs * g, axis=-1, keepdims=True))).astype(BF16)
        dqn = jnp.dot(ds, k, preferred_element_type=F32) * SCALE
        dkn = dot_first(ds, q) * SCALE
        out[left(1)] = norm_backward(dqn, qhat, qinv).astype(BF16)
        out[right(1)] = norm_backward(dkn, khat, kinv).astype(BF16)
        out[left(2)] = dot_first(half, datt).astype(BF16)


def gather_kernel(
    down, inp, cot, unit, inv, tri, exp, mer, shr, outputs, block_grad, ring,
    held, slots, acc, xsend, xgot, stat_out, stat_in,
    wsem, zs, zr, ys, yr, cs, cr, xs, xr, ss, sr,
):
    r, m, x, y, z, c = place()
    refs = {"t": tri, "e": exp, "m": mer, "s": shr}
    peers = partners(m, y, z, c)
    xpeers = [(x + i) % 4 for i in (1, 2, 3)]
    inner = m % 8
    up = {"dp": (r + z) % 4, "mx": inner + 8 * (1 - z)}
    below = {"dp": (r + 3 + z) % 4, "mx": inner + 8 * (1 - z)}
    greet([up, below] + [{"mx": peers[q]} for q in (0, 1, 3)] + [{"my": q} for q in xpeers])

    top, bottom = pl.ds(0, 128), pl.ds(128, 128)

    def hop(k, way):
        sem = (zs.at[way, k], zr.at[way, k])
        if way == 0:
            src = down if k == 0 else ring.at[8 - k]
            dst = ring.at[7 - k]
            if k == 3:
                src, dst = src.at[:, top], dst.at[:, top]
            return remote(src, dst, *sem, up)
        src = down if k == 0 else ring.at[k]
        dst = ring.at[k + 1]
        if k == 3:
            src, dst = src.at[:, bottom], dst.at[:, bottom]
        return remote(src, dst, *sem, below)

    def y_send(dz, k):
        src = down if dz == 0 else ring.at[1 + 6 * z]
        sem = (ys.at[dz, k], yr.at[dz, k])
        if k == 0:
            return remote(src, slots.at[dz, 2, 0], *sem, {"mx": peers[0]})
        if k == 1:
            return remote(src, slots.at[dz, 1, 0], *sem, {"mx": peers[1]})
        if k == 2:
            return remote(slots.at[dz, 2, 0, :, top], slots.at[dz, 3, 0, :, top], *sem, {"mx": peers[1]})
        return remote(slots.at[dz, 1, 0, :, bottom], slots.at[dz, 3, 0, :, bottom], *sem, {"mx": peers[0]})

    def core_send(dz, ab):
        src = slots.at[dz, ab, 0]
        if ab == 0:
            src = down if dz == 0 else ring.at[1 + 6 * z]
        return remote(src, slots.at[dz, ab, 1], cs.at[dz, ab], cr.at[dz, ab], {"mx": peers[3]})

    hop(0, 0).start()
    hop(0, 1).start()
    y_send(0, 0).start()
    y_send(0, 1).start()
    core_send(0, 0).start()
    for p in range(3):
        load_weights(p, refs, held, wsem, y, z, c)
    ring[0] = down[...]
    acc[...] = jnp.zeros_like(acc)
    for p in range(3):
        wait_weights(p, held, wsem)

    def multiply(data, dz, ab, dc):
        s = ab * 4 + dz * 2 + dc
        fourth = ((z + dz) % 2) * ((c + dc) % 2)
        acc[0] += dot_last(data[0], held[0, s])
        acc[1] += dot_last(data[1, :, 128:256], held[1, s, :, 128:256]) + dot_last(data[2], held[2, s])
        acc[1 - fourth] += dot_last(data[1, :, 0:128], held[1, s, :, 0:128])

    def take(dz, ab):
        core_send(dz, ab).start()
        multiply(slots.at[dz, ab, 0], dz, ab, 0)

    def take_other(dz, ab):
        core_send(dz, ab).wait_recv()
        multiply(slots.at[dz, ab, 1], dz, ab, 1)

    multiply(down, 0, 0, 0)
    hop(0, 0).wait_recv()
    hop(0, 1).wait_recv()
    hop(1, 0).start()
    hop(1, 1).start()
    y_send(1, 0).start()
    y_send(1, 1).start()
    core_send(1, 0).start()
    y_send(0, 0).wait_recv()
    y_send(0, 2).start()
    y_send(0, 1).wait_recv()
    y_send(0, 3).start()
    take(0, 2)
    take(0, 1)
    multiply(ring.at[1 + 6 * z], 1, 0, 0)
    take_other(0, 0)
    hop(1, 0).wait_recv()
    hop(1, 1).wait_recv()
    hop(2, 0).start()
    hop(2, 1).start()
    take_other(1, 0)
    y_send(1, 0).wait_recv()
    y_send(1, 2).start()
    y_send(1, 1).wait_recv()
    y_send(1, 3).start()
    y_send(0, 2).wait_recv()
    y_send(0, 3).wait_recv()
    take(0, 3)
    take(1, 2)
    take(1, 1)
    hop(2, 0).wait_recv()
    hop(2, 1).wait_recv()
    hop(3, 0).start()
    hop(3, 1).start()
    for ab in (2, 1, 3):
        take_other(0, ab)
    y_send(1, 2).wait_recv()
    y_send(1, 3).wait_recv()
    take(1, 3)
    for ab in (2, 1, 3):
        take_other(1, ab)

    xsend[...] = acc[...].astype(BF16)

    def x_send(i):
        rows_of = pl.ds(pl.multiple_of(xpeers[i] * 64, 64), 64)
        return remote(xsend.at[:, rows_of], xgot.at[i], xs.at[i], xr.at[i], {"my": xpeers[i]})

    for i in range(3):
        x_send(i).start()
    own = pl.ds(pl.multiple_of(x * 64, 64), 64)
    branch = acc[0, own, :]
    grad = acc[1, own, :]
    for i in range(3):
        x_send(i).wait_recv()
        branch = branch + xgot[i, 0].astype(F32)
        grad = grad + xgot[i, 1].astype(F32)
    outputs[...] = (inp[...].astype(F32) + branch).astype(BF16)
    hat = unit[...]
    first = jnp.sum(grad, axis=1, keepdims=True)
    second = jnp.sum(grad * hat, axis=1, keepdims=True)
    low = lax.broadcasted_iota(jnp.int32, (64, 128), 1) < 64
    for step in range(4):
        stat_out[step] = jnp.where(low, first, second)
        copy = remote(
            stat_out.at[step], stat_in.at[step], ss.at[step], sr.at[step], {"mx": peers[(3, 0, 1, 2)[step]]}
        )
        copy.start()
        copy.wait()
        other = stat_in[step]
        first = first + other[:, 0:1]
        second = second + other[:, 64:65]
    fixed = (grad - first / WIDTH - hat * (second / WIDTH)) * inv[:, 0:1]
    block_grad[...] = (cot[...].astype(F32) + fixed).astype(BF16)

    hop(3, 0).wait_recv()
    hop(3, 1).wait_recv()
    for k in range(4):
        for way in range(2):
            hop(k, way).wait_send()
    for dz in range(2):
        for k in range(4):
            y_send(dz, k).wait_send()
            core_send(dz, k).wait_send()
    for i in range(3):
        x_send(i).wait_send()


def weight_kernel(ring, rows, tri, exp, mer, shr, left, res, got, lsem, osem, gs, gr):
    r, m, x, y, z, c = place()
    me = m % 8
    refs = {"t": tri, "e": exp, "m": mer, "s": shr}
    others = [(me + i) % 8 for i in range(1, 8)]
    for q in range(8):
        pltpu.make_async_copy(rows.at[q], left.at[:, :, pl.ds(96 * q, 96)], lsem).start()
    greet([{"mx": q + 8 * z} for q in others])
    pltpu.make_async_copy(left, left, lsem).wait()

    def result(dz, p, i):
        q = others[i]
        return remote(
            res.at[dz, p, q], got.at[dz, p, me], gs.at[dz, p, i], gr.at[dz, p, i], {"mx": q + 8 * z}
        )

    for dz in range(2):
        zo = (z + dz) % 2
        fourth = zo * c
        for p in range(3):
            def pick(k):
                d = (dz * (1 + 6 * z) + 2 * k) % 8
                return (r + (k if dz else k)) % 4, d

            def total(side, columns):
                acc = None
                for k in range(4):
                    rep, d = pick(k)
                    term = jnp.dot(left[side, rep], ring[d, p, :, columns], preferred_element_type=F32)
                    acc = term if acc is None else acc + term
                return acc.astype(BF16).reshape(8, 96, -1)

            if p == 1:
                res[dz, p, :, :, 0:128] = total(fourth, slice(0, 128))
                res[dz, p, :, :, 128:256] = total(0, slice(128, 256))
            else:
                res[dz, p] = total(1 if p == 0 else 0, slice(0, 256))
            got[dz, p, me] = res[dz, p, me]
            for i in range(7):
                result(dz, p, i).start()

    for dz in range(2):
        for p in range(3):
            for i in range(7):
                result(dz, p, i).wait_recv()

            def store(q, carry):
                fourth, usual, last = share_columns(q // 2, (z + dz) % 2, q % 2)

                def start(blocks):
                    for half in range(2):
                        name, index = blocks[2 * p + half]
                        pltpu.make_async_copy(
                            got.at[dz, p, q, :, pl.ds(128 * half, 128)], refs[name].at[:, lanes(index)], osem
                        ).start()

                @pl.when(fourth)
                def _():
                    start(last)

                @pl.when(jnp.logical_not(fourth))
                def _():
                    start(usual)

                return carry

            lax.fori_loop(0, 8, store, 0)
    for dz in range(2):
        for p in range(3):
            for i in range(7):
                result(dz, p, i).wait_send()
    pltpu.make_async_copy(got, got, osem).wait()


def params(number=None):
    if number is None:
        return pltpu.CompilerParams(vmem_limit_bytes=VMEM_LIMIT)
    return pltpu.CompilerParams(collective_id=number, has_side_effects=True, vmem_limit_bytes=VMEM_LIMIT)


VM = pl.BlockSpec(memory_space=pltpu.VMEM)
HB = pl.BlockSpec(memory_space=pl.ANY)
SEM = pltpu.SemaphoreType.DMA


def shape(*dims, dtype=BF16):
    return jax.ShapeDtypeStruct(dims, dtype)


def project(inp, cot, tri, exp, mer, shr):
    return pl.pallas_call(
        project_kernel,
        out_shape=(
            shape(3, 256, 256, dtype=F32), shape(64, 384), shape(256, 384), shape(256, 384),
            shape(64, 384, dtype=F32), shape(64, 128, dtype=F32),
        ),
        in_specs=[VM, VM, HB, HB, HB, HB],
        out_specs=(VM,) * 6,
        scratch_shapes=[
            pltpu.VMEM((3, 16, 384, 256), BF16),
            pltpu.VMEM((3, 2, 8, 256, 256), BF16),
            pltpu.VMEM((3, 8, 256, 256), BF16),
            pltpu.VMEM((3, 4, 256, 256), BF16),
            pltpu.VMEM((3, 2, 256, 256), BF16),
            pltpu.VMEM((3, 1, 256, 256), BF16),
            pltpu.VMEM((4, 64, 128), F32),
            pltpu.VMEM((4, 64, 128), F32),
            pltpu.VMEM((2, 256, 384), BF16),
            SEM((3,)), SEM((2, 3)), SEM((2, 3)), SEM((4,)), SEM((4,)), SEM((3, 4)), SEM((3, 4)),
        ],
        compiler_params=params(0),
        name="project",
    )(inp, cot, tri, exp, mer, shr)


def middle(proj):
    return pl.pallas_call(
        middle_kernel,
        out_shape=shape(3, 256, 256),
        in_specs=[VM],
        out_specs=VM,
        compiler_params=params(),
        name="middle",
    )(proj)


def gather(down, inp, cot, unit, inv, tri, exp, mer, shr):
    return pl.pallas_call(
        gather_kernel,
        out_shape=(shape(64, 384), shape(64, 384), shape(8, 3, 256, 256)),
        in_specs=[VM] * 5 + [HB] * 4,
        out_specs=(VM,) * 3,
        scratch_shapes=[
            pltpu.VMEM((3, 16, 384, 256), BF16),
            pltpu.VMEM((2, 4, 2, 3, 256, 256), BF16),
            pltpu.VMEM((2, 256, 384), F32),
            pltpu.VMEM((2, 256, 384), BF16),
            pltpu.VMEM((3, 2, 64, 384), BF16),
            pltpu.VMEM((4, 64, 128), F32),
            pltpu.VMEM((4, 64, 128), F32),
            SEM((3,)), SEM((2, 4)), SEM((2, 4)), SEM((2, 4)), SEM((2, 4)), SEM((2, 4)), SEM((2, 4)),
            SEM((3,)), SEM((3,)), SEM((4,)), SEM((4,)),
        ],
        compiler_params=params(1),
        name="gather",
    )(down, inp, cot, unit, inv, tri, exp, mer, shr)


def weight_grads(ring, rows):
    return pl.pallas_call(
        weight_kernel,
        out_shape=(shape(96, 4608), shape(96, 3072), shape(96, 1536), shape(96, 3072)),
        in_specs=[VM, HB],
        out_specs=(HB,) * 4,
        scratch_shapes=[
            pltpu.VMEM((2, 4, 768, 256), BF16),
            pltpu.VMEM((2, 3, 8, 96, 256), BF16),
            pltpu.VMEM((2, 3, 8, 96, 256), BF16),
            SEM(()), SEM(()), SEM((2, 3, 7)), SEM((2, 3, 7)),
        ],
        compiler_params=params(2),
        name="weights",
    )(ring, rows)


def row_shares(normed, cot):
    pair = jnp.stack([normed, cot])
    all_reps = lax.all_gather(pair, "dp")
    mine = lax.dynamic_slice_in_dim(all_reps, lax.axis_index("dp") * 96, 96, axis=3)
    turned = mine.transpose(1, 0, 3, 2)
    wide = lax.all_gather(turned, "my", axis=3, tiled=True)
    return lax.all_gather(wide, "mx", axis_index_groups=[list(range(8)), list(range(8, 16))])


def body(inputs, triple_weight, expand_weight, merge_weight, shrink_weight, cotangent):
    tri = triple_weight.reshape(triple_weight.shape[0], -1)
    weights = (tri, expand_weight, merge_weight, shrink_weight)
    proj, normed, nfull, cfull, unit, inv = project(inputs, cotangent, *weights)
    rows = row_shares(normed, cotangent)
    down = middle(proj)
    outputs, block_grad, ring = gather(down, inputs, cotangent, unit, inv, *weights)
    tg, eg, mg, sg = weight_grads(ring, rows)
    return outputs, block_grad, tg.reshape(96, 3, -1), eg, mg, sg


def solution(mesh):
    placed = (
        P(("dp", "my"), "mx"),
        P("mx", None, "my"),
        P("mx", "my"),
        P("mx", "my"),
        P("mx", "my"),
        P(("dp", "my"), "mx"),
    )
    return jax.shard_map(
        body,
        mesh=mesh,
        in_specs=placed,
        out_specs=(
            P(("dp", "my"), "mx"),
            P(("dp", "my"), "mx"),
            P(("mx", "dp"), None, "my"),
            P(("mx", "dp"), "my"),
            P(("mx", "dp"), "my"),
            P(("mx", "dp"), "my"),
        ),
        check_vma=False,
    )
```

time: 865 us -> 224 us (0.26)
  waiting for transfers between devices: 595 us -> 0.04 us
  Pallas kernels: 0 us -> 164 us
  blocking collectives: 143 us -> 27.8 us
  matrix products: 55 us -> 0 us
  other arithmetic: 19.5 us -> 0.81 us
  local copies, waits for them, and re-layouts: 34.6 us -> 16.6 us
    reduce_scatter x10 -> x0, waiting for transfers between devices: 422 us -> none  [the longest x2 129 us: sum_rows(): lax.psum_scatter(pair[1].astype(jnp.bfloat16), 'mx', scatter_dimension=0,...]
    pallas_call x0 -> x4, Pallas kernels: none -> 164 us  [the longest x1 68.4 us: gather(): pl.pallas_call(gather_kernel, out_shape=(shape(64, 384), shape(64, 384),...]
    unnamed x17 -> x1, waiting for transfers between devices: 92.7 us -> 0.02 us
    all_gather x3 -> x1, waiting for transfers between devices: 80 us -> 0.02 us  [row_shares(): lax.all_gather(wide, 'mx', axis_index_groups=[list(range(8)), list(range(...]
    all_gather x5 -> x2, blocking collectives: 86 us -> 27.8 us  [the longest x1 17.5 us: row_shares(): all_reps = lax.all_gather(pair, 'dp')]
    psum x2 -> x0, blocking collectives: 57.3 us -> none  [row_totals(): return lax.psum((pair[0], pair[1]), 'mx')]
    dot_general x17 -> x0, matrix products: 52.1 us -> none  [the longest x4 14.5 us: contract_last(): lax.dot_general(left, right, (((1,), (1,)), ((), ())), preferred_element_...]
  transfers between devices with their start and end apart: 15 -> 1, of which waited for: 13 -> 0; matrix products, arithmetic and copies ran while one was open for 10% -> 0% of each run, Pallas kernels for 0% -> 32%
where the time goes in v1:
time: 224 us; the launch traced here: 223 us
  Pallas kernels  164 us (73%)
  blocking collectives  27.8 us (12%)
  local copies, waits for them, and re-layouts  16.6 us (7%)
  between operations  14.1 us (6%)
    pallas_call x1, Pallas kernels, gather(): pl.pallas_call(gather_kernel, out_shape=(shape(64, 384), shape(64, 384),...  68.4 us
    pallas_call x1, Pallas kernels, project(): pl.pallas_call(project_kernel, out_shape=(shape(3, 256, 256, dtype=F32),...  56.3 us
    pallas_call x1, Pallas kernels, weight_grads(): pl.pallas_call(weight_kernel, out_shape=(shape(96, 4608), shape(96, 3072)...  36.2 us
    all_gather x1, blocking collectives, row_shares(): all_reps = lax.all_gather(pair, 'dp')  17.5 us
    all_gather x1, blocking collectives, row_shares(): wide = lax.all_gather(turned, 'my', axis=3, tiled=True)  10.3 us
    unnamed x17, local copies, waits for them, and re-layouts  9.35 us
  transfers between devices with their start and end apart: 1, of which 0 were waited for; matrix products, arithmetic and copies ran while one was open for 0% of the time, Pallas kernels for 32%

profile of v1, /device:TPU:1, one launch (start us, length us, event | category | flops | bytes accessed | tf_op | source)
XLA Modules:
  0.0 223.5 jit_solution(4231095192360763489)
XLA Ops:
  7.2 0.0 all-gather.4.cloned.1.call-start
  7.2 4.5 %copy.20 = bf16[384,3,1536]{0,2,1:T(8,128)(2,1)S(1)} copy(bf16[384,3,1536]{2,0,1:T(8,128)(2,1)} %param.7) | data formatting | bytes 7077888 | tf_op args[1]
  11.8 3.8 %copy.21.tri = bf16[384,4608]{1,0:T(8,128)(2,1)} copy(bf16[384,4608]{0,1:T(8,128)(2,1)S(1)} %bitcast.12) | data formatting | bytes 7077888 | tf_op jit(solution)/shard_map/reshape | solution.py:646
  15.6 0.0 copy-start.1
  15.6 56.3 %project.1 = (f32[3,256,256]{2,1,0:T(8,128)}, bf16[64,384]{1,0:T(8,128)(2,1)}, bf16[256,384]{1,0:T(8,128)(2,1)}, bf16[256,384]{1,0:T(8,128)(2,1)}, f32[64,384]{1,0:T(8,128)}, /*index=5*/f32[64,128]{1,0:T(8,128)}) custom-call(bf16[64,384]{1,0:T(8,128)(2,1)} %inp.3, bf16[64,384]{1,0:T(8,128)(2,1)} %cot.3, bf16[384,4608]{1,0:T(8,128)(2,1)} %copy.21.tri, ...), custom_call_target="tpu_custom_call" | custom-call | tf_op jit(solution)/shard_map/project/pallas_call | solution.py:561
  71.9 0.0 copy-done.1
  71.9 0.8 pad_maximum_fusion
  72.7 17.5 %all-gather = bf16[8,64,384]{2,1,0:T(8,128)(2,1)S(1)} all-gather(bf16[2,64,384]{2,1,0:T(8,128)(2,1)S(1)} %pad_maximum_fusion), channel_id=2, replica_groups=mesh['dp'=4,'mx'=16,'my'=4] {'dp'}, dimensions={0}, use_global_device_ids=true | all-gather | bytes 491520 | tf_op jit(solution)/shard_map/all_gather | solution.py:638
  90.2 0.1 constant_dynamic-slice_fusion
  90.3 0.1 copy.31
  90.4 10.3 %all_gather.17 = bf16[2,4,96,256]{2,1,0,3:T(4,128)(2,1)S(1)} all-gather(bf16[2,4,96,64]{2,1,0,3:T(4,128)(2,1)S(1)} %bitcast.17), channel_id=1, replica_groups=mesh['dp'=4,'mx'=16,'my'=4] {'my'}, dimensions={3}, use_global_device_ids=true | all-gather | bytes 491520 | tf_op jit(solution)/shard_map/all_gather | solution.py:641
  100.7 1.1 copy.24
  101.8 0.0 all-gather.4.cloned.1.call-update
  101.8 3.2 %middle.1.down = bf16[3,256,256]{2,1,0:T(8,128)(2,1)} custom-call(f32[3,256,256]{2,1,0:T(8,128)} %get-tuple-element.17.proj), custom_call_target="tpu_custom_call" | custom-call | tf_op jit(solution)/shard_map/middle/pallas_call | solution.py:587
  105.0 68.4 %gather.1 = (bf16[64,384]{1,0:T(8,128)(2,1)}, bf16[64,384]{1,0:T(8,128)(2,1)}, bf16[8,3,256,256]{3,2,1,0:T(8,128)(2,1)}) custom-call(bf16[3,256,256]{2,1,0:T(8,128)(2,1)} %middle.1.down, bf16[64,384]{1,0:T(8,128)(2,1)} %inp.3, bf16[64,384]{1,0:T(8,128)(2,1)} %cot.3, f32[64,384]{1,0:T(8,128)} %get-tuple-element.18.unit, f32[64,128]{1,0:T(8,128)} %get-tuple-element.19.inv, ...), custom_call_target="tpu_custom_call" | custom-call | tf_op jit(solution)/shard_map/gather/pallas_call | solution.py:598
  173.4 0.0 all-gather.4.cloned.1.call-done
  173.4 0.0 copy-start.4
  173.4 0.0 copy-start.3
  173.5 36.2 %weights.1 = (bf16[96,4608]{1,0:T(8,128)(2,1)}, bf16[96,3072]{1,0:T(8,128)(2,1)}, bf16[96,1536]{1,0:T(8,128)(2,1)}, bf16[96,3072]{1,0:T(8,128)(2,1)}) custom-call(bf16[8,3,256,256]{3,2,1,0:T(8,128)(2,1)} %get-tuple-element.22.ring, bf16[8,2,4,96,256]{4,3,2,1,0:T(8,128)(2,1)} %bitcast.13), custom_call_target="tpu_custom_call" | custom-call | tf_op jit(solution)/shard_map/weights/pallas_call | solution.py:620
  209.7 0.0 copy-start.2
  209.7 0.0 copy-start
  209.7 2.2 %copy.30 = bf16[12,3,8,1536]{3,2,0,1:T(8,128)(2,1)} copy(bf16[12,3,8,1536]{3,2,1,0:T(8,128)(2,1)} %bitcast.15) | data formatting | bytes 1769472 | tf_op jit(solution)/shard_map/reshape | solution.py:653
  211.9 0.0 copy-done.4
  211.9 0.6 copy.37
  212.6 0.0 copy-done.3
  212.6 0.6 copy.38
  213.2 1.9 copy.39
  215.1 0.0 copy-done.2
  215.1 0.7 copy.40
  215.8 0.0 copy-done
  215.8 0.8 copy.41
Async XLA Ops:
  7.2 166.3 %all-gather.4.cloned.1.call-start = ((), (), s32[]{:S(2)}) async-start(), calls=%async_computation | async-start | bytes 3538944 | tf_op jit(solution)/shard_map/all_gather | solution.py:642
  15.6 56.3 %copy-start.1 = (bf16[64,384]{1,0:T(8,128)(2,1)S(1)}, bf16[64,384]{1,0:T(8,128)(2,1)}, u32[]{:S(2)}) copy-start(bf16[64,384]{1,0:T(8,128)(2,1)} %cot.3) | copy-start | bytes 147460
  173.4 38.5 %copy-start.4 = (bf16[64,384]{1,0:T(8,128)(2,1)S(1)}, bf16[64,384]{1,0:T(8,128)(2,1)}, u32[]{:S(2)}) copy-start(bf16[64,384]{1,0:T(8,128)(2,1)} %get-tuple-element.52) | copy-start | bytes 147460
  173.4 39.1 %copy-start.3 = (bf16[64,384]{1,0:T(8,128)(2,1)S(1)}, bf16[64,384]{1,0:T(8,128)(2,1)}, u32[]{:S(2)}) copy-start(bf16[64,384]{1,0:T(8,128)(2,1)} %get-tuple-element.53) | copy-start | bytes 147460
  209.7 5.4 %copy-start.2 = (bf16[96,1536]{1,0:T(8,128)(2,1)S(1)}, bf16[96,1536]{1,0:T(8,128)(2,1)}, u32[]{:S(2)}) copy-start(bf16[96,1536]{1,0:T(8,128)(2,1)} %get-tuple-element.56) | copy-start | bytes 884740
  209.7 6.1 %copy-start = (bf16[96,3072]{1,0:T(8,128)(2,1)S(1)}, bf16[96,3072]{1,0:T(8,128)(2,1)}, u32[]{:S(2)}) copy-start(bf16[96,3072]{1,0:T(8,128)(2,1)} %get-tuple-element.57) | copy-start | bytes 1769476
Sparse Core Ops, SparseCore 0:
  102.0 46.0 all-gather.3

commit v2 on v1

v2 whole, which is shorter than its diff:
```python
import functools
import math

import jax
import jax.numpy as jnp
from jax import lax
from jax.experimental import pallas as pl
from jax.experimental.pallas import tpu as pltpu
from jax.sharding import PartitionSpec as P

MESH = pl.DeviceIdType.MESH
F32 = jnp.float32
BF16 = jnp.bfloat16

WIDTH = 6144
EPS = 1e-06
ROOT_HALF = 0.7071067811865476
INV_ROOT_TAU = 0.3989422804014327
SCALE = 1.0 / math.sqrt(128)
VMEM_LIMIT = 56 * 1024 * 1024

SEQ = ((0, 1, 2), (1, 2, 0), (2, 0, 1))
CUTS = (((0, 96), (96, 80), (176, 80)), ((0, 80), (80, 96), (176, 80)), ((0, 80), (80, 80), (160, 96)))


def place():
    m = lax.axis_index("mx")
    c = m % 2
    y = (m // 2) % 4
    z = m // 8
    return lax.axis_index("dp"), m, lax.axis_index("my"), y, z, c


def partners(m, y, z, c):
    return (m + 2 * (1 - 2 * (y % 2)), m + 2 * (3 - 2 * y), m + 8 - 16 * z, m + 1 - 2 * c)


def owner_of(y, z, c, da, db, dz, dc):
    b = (y // 2 + db) % 2
    a = (y + y // 2 + da) % 2
    return 2 * b + (a + b) % 2, (z + dz) % 2, (c + dc) % 2


def share_columns(yo, zo, co):
    k = zo * 2 + co
    head = 3 * yo + k
    unit = 6 * yo + k
    usual = (("m", head), ("s", unit), ("q", head), ("k", head), ("v", head), ("e", unit))
    first = 6 * yo + 3
    fourth = (("s", first), ("s", first + 1), ("s", first + 2), ("e", first), ("e", first + 1), ("e", first + 2))
    return k == 3, usual, fourth


def named(tri, exp, mer, shr):
    return {"q": tri.at[0], "k": tri.at[1], "v": tri.at[2], "e": exp, "m": mer, "s": shr}


def lanes(index):
    return pl.ds(pl.multiple_of(index * 128, 128), 128)


def load_weights(p, refs, held, sem, y, z, c):
    def step(s, carry):
        yo, zo, co = owner_of(y, z, c, s // 8, (s // 4) % 2, (s // 2) % 2, s % 2)
        fourth, usual, last = share_columns(yo, zo, co)

        def start(blocks):
            for half in range(2):
                name, index = blocks[2 * p + half]
                pltpu.make_async_copy(
                    refs[name].at[:, lanes(index)], held.at[p, s, :, pl.ds(128 * half, 128)], sem.at[p]
                ).start()

        @pl.when(fourth)
        def _():
            start(last)

        @pl.when(jnp.logical_not(fourth))
        def _():
            start(usual)

        return carry

    lax.fori_loop(0, 16, step, 0)


def wait_weights(p, held, sem):
    pltpu.make_async_copy(held.at[p], held.at[p], sem.at[p]).wait()


def remote(src, dst, send, recv, device):
    return pltpu.make_async_remote_copy(
        src_ref=src, dst_ref=dst, send_sem=send, recv_sem=recv, device_id=device, device_id_type=MESH
    )


def greet(devices):
    barrier = pltpu.get_barrier_semaphore()
    for device in devices:
        pl.semaphore_signal(barrier, inc=1, device_id=device, device_id_type=MESH)
    pl.semaphore_wait(barrier, len(devices))


def dot_last(left, right):
    return lax.dot_general(left, right, (((1,), (1,)), ((), ())), preferred_element_type=F32)


def dot_first(left, right):
    return lax.dot_general(left, right, (((0,), (0,)), ((), ())), preferred_element_type=F32)


def project_kernel(
    inp, cot, tri, exp, mer, shr, out, unit_out, inv_out, spread,
    held, part, got0, got1, got2, got3, stat_out, stat_in, nown, both, turned, mixed,
    wsem, xs, xr, ss, sr, rs, rr, es, er, fs, fr,
):
    r, m, x, y, z, c = place()
    refs = named(tri, exp, mer, shr)
    peers = partners(m, y, z, c)
    xpeers = [(x + i) % 4 for i in (1, 2, 3)]
    rpeers = [(r + i) % 4 for i in (1, 2, 3)]
    greet([{"my": q} for q in xpeers] + [{"mx": q} for q in peers] + [{"dp": q} for q in rpeers])

    own = pl.ds(pl.multiple_of(x * 64, 64), 64)
    sends = []
    for i in range(3):
        copy = remote(cot, both.at[1, own], xs.at[0, i], xr.at[0, i], {"my": xpeers[i]})
        copy.start()
        sends.append(copy)
    both[1, own, :] = cot[...]

    rows = inp[...].astype(F32)
    mean = jnp.sum(rows, axis=1, keepdims=True) / rows.shape[1]
    centred = rows - mean
    square = jnp.sum(centred * centred, axis=1, keepdims=True)
    low = lax.broadcasted_iota(jnp.int32, (64, 128), 1) < 64
    stats = [mean, square, float(rows.shape[1])]

    def stat_copy(step):
        return remote(
            stat_out.at[step], stat_in.at[step], ss.at[step], sr.at[step], {"mx": peers[(3, 0, 1, 2)[step]]}
        )

    def stat_start(step):
        stat_out[step] = jnp.where(low, stats[0], stats[1])
        stat_copy(step).start()

    def stat_finish(step):
        stat_copy(step).wait_recv()
        other = stat_in[step]
        mean2, square2 = other[:, 0:1], other[:, 64:65]
        delta = mean2 - stats[0]
        stats[1] = stats[1] + square2 + delta * delta * (stats[2] / 2)
        stats[0] = (stats[0] + mean2) * 0.5
        stats[2] = stats[2] * 2

    stat_start(0)
    load_weights(0, refs, held, wsem, y, z, c)
    stat_finish(0)
    stat_start(1)

    def gathered(k):
        for i in range(3):
            rows_of = both.at[1 - k, pl.ds(pl.multiple_of(((x + 3 - i) % 4) * 64, 64), 64)]
            remote(rows_of, rows_of, xs.at[k, i], xr.at[k, i], {"my": xpeers[i]}).wait_recv()

    def multiply(p, dc):
        def step(t, carry):
            da, db, dz = t // 4, (t // 2) % 2, t % 2
            s = t * 2 + dc
            places = (t, 4 * db + 2 * dz + da, 4 * dz + 2 * da + db)

            def put(value, columns):
                for q in range(3):
                    at, size = CUTS[p][q]
                    part[p, q, dc, places[q], 0:size, columns] = value[at : at + size]

            if p == 1:
                fourth = ((z + dz) % 2) * ((c + dc) % 2)
                first = jnp.dot(both[fourth], held[p, s, :, 0:128], preferred_element_type=F32)
                second = jnp.dot(both[0], held[p, s, :, 128:256], preferred_element_type=F32)
                put(first.astype(BF16), slice(0, 128))
                put(second.astype(BF16), slice(128, 256))
            else:
                full = both[1 if p == 0 else 0]
                put(jnp.dot(full, held[p, s], preferred_element_type=F32).astype(BF16), slice(0, 256))
            return carry

        lax.fori_loop(0, 8, step, 0)

    def stage(p, q, k):
        size = CUTS[p][q][1]
        sem = (rs.at[p, q, k], rr.at[p, q, k])
        if k == 0:
            return remote(part.at[p, q, 1, :, 0:size], got0.at[p, q, :, 0:size], *sem, {"mx": peers[3]})
        slots = 8 >> k
        target = (None, got1, got2, got3)[k]
        return remote(
            part.at[p, q, 0, pl.ds(slots, slots), 0:size], target.at[p, q, :, 0:size], *sem,
            {"mx": peers[SEQ[q][k - 1]]},
        )

    def begin(p):
        for q in range(3):
            stage(p, q, 0).start()

    def advance(p, k):
        source = (got0, got1, got2, got3)[k]
        for q in range(3):
            at, size = CUTS[p][q]
            stage(p, q, k).wait_recv()

            def step(t, carry):
                total = part[p, q, 0, t, 0:size].astype(F32) + source[p, q, t, 0:size].astype(F32)
                part[p, q, 0, t, 0:size] = total.astype(BF16)
                return carry

            if k < 3:
                lax.fori_loop(0, 8 >> k, step, 0)
                stage(p, q, k + 1).start()
            else:
                out[p, at : at + size] = (
                    part[p, q, 0, 0, 0:size].astype(F32) + source[p, q, 0, 0:size].astype(F32)
                )

    gathered(0)
    wait_weights(0, held, wsem)
    multiply(0, 1)
    begin(0)
    stat_finish(1)
    stat_start(2)
    multiply(0, 0)
    stat_finish(2)
    stat_start(3)
    advance(0, 0)
    load_weights(1, refs, held, wsem, y, z, c)
    stat_finish(3)
    mean, square = stats[0], stats[1]
    inverse = lax.rsqrt(square / WIDTH + EPS)
    unit = (rows - mean) * inverse
    nown[...] = unit.astype(BF16)
    both[0, own, :] = unit.astype(BF16)
    for i in range(3):
        copy = remote(nown, both.at[0, own], xs.at[1, i], xr.at[1, i], {"my": xpeers[i]})
        copy.start()
        sends.append(copy)
    unit_out[...] = unit
    inv_out[...] = jnp.broadcast_to(inverse, (64, 128))
    load_weights(2, refs, held, wsem, y, z, c)
    advance(0, 1)
    gathered(1)
    wait_weights(1, held, wsem)
    multiply(1, 1)
    begin(1)
    multiply(1, 0)
    advance(1, 0)
    wait_weights(2, held, wsem)
    multiply(2, 1)
    begin(2)
    multiply(2, 0)
    advance(0, 2)
    advance(2, 0)

    quarter = both[x // 2, pl.ds(pl.multiple_of((x % 2) * 128, 128), 128), :]
    turned[...] = quarter.T.reshape(4, 96, 128)

    def swap(i):
        q = rpeers[i]
        return remote(turned.at[q], mixed.at[3 - i], es.at[i], er.at[i], {"dp": q})

    def pass_on(k):
        sem = (fs.at[k], fr.at[k])
        if k == 0:
            return remote(mixed, spread.at[:, 2], *sem, {"mx": peers[0]})
        if k == 1:
            return remote(mixed, spread.at[:, 1], *sem, {"mx": peers[1]})
        if k == 2:
            return remote(spread.at[0:2, 2], spread.at[0:2, 3], *sem, {"mx": peers[1]})
        return remote(spread.at[2:4, 1], spread.at[2:4, 3], *sem, {"mx": peers[0]})

    for i in range(3):
        swap(i).start()
    mixed[0] = turned[r]
    advance(1, 1)
    advance(2, 1)
    for i in range(3):
        swap(i).wait_recv()
    pass_on(0).start()
    pass_on(1).start()
    spread[:, 0] = mixed[...]
    advance(1, 2)
    advance(2, 2)
    pass_on(0).wait_recv()
    pass_on(2).start()
    pass_on(1).wait_recv()
    pass_on(3).start()
    for p in range(3):
        advance(p, 3)
    pass_on(2).wait_recv()
    pass_on(3).wait_recv()
    for copy in sends:
        copy.wait_send()
    for step in range(4):
        stat_copy(step).wait_send()
        pass_on(step).wait_send()
    for i in range(3):
        swap(i).wait_send()
    for p in range(3):
        for q in range(3):
            for k in range(4):
                stage(p, q, k).wait_send()


def norm_heads(block):
    centre = block - jnp.mean(block, axis=-1, keepdims=True)
    inverse = lax.rsqrt(jnp.mean(centre * centre, axis=-1, keepdims=True) + EPS)
    return centre * inverse, inverse


def norm_backward(grad, unit, inverse):
    first = jnp.mean(grad, axis=-1, keepdims=True)
    second = jnp.mean(grad * unit, axis=-1, keepdims=True)
    return (grad - first - unit * second) * inverse


def gelu_pair(pre):
    phi = 0.5 * (1.0 + lax.erf(pre * ROOT_HALF))
    return pre * phi, phi + pre * jnp.exp(-0.5 * pre * pre) * INV_ROOT_TAU


def middle_kernel(proj, out):
    r, m, x, y, z, c = place()
    fourth = z * 2 + c == 3

    def left(p):
        return (p, slice(None), slice(0, 128))

    def right(p):
        return (p, slice(None), slice(128, 256))

    def unit(pre_at, grad_at):
        value, slope = gelu_pair(proj[pre_at])
        grad = proj[grad_at]
        out[grad_at] = value.astype(BF16)
        out[pre_at] = (grad * slope).astype(BF16)

    @pl.when(fourth)
    def _():
        unit(right(1), left(0))
        unit(left(2), right(0))
        unit(right(2), left(1))

    @pl.when(jnp.logical_not(fourth))
    def _():
        unit(right(2), right(0))
        qhat, qinv = norm_heads(proj[left(1)])
        khat, kinv = norm_heads(proj[right(1)])
        q, k = qhat.astype(BF16), khat.astype(BF16)
        v = proj[left(2)].astype(BF16)
        datt = proj[left(0)].astype(BF16)
        expo = jnp.exp(dot_last(q, k) * SCALE)
        probs = expo / jnp.sum(expo, axis=-1, keepdims=True)
        half = probs.astype(BF16)
        out[left(0)] = jnp.dot(half, v, preferred_element_type=F32).astype(BF16)
        g = dot_last(datt, v)
        ds = (probs * (g - jnp.sum(probs * g, axis=-1, keepdims=True))).astype(BF16)
        dqn = jnp.dot(ds, k, preferred_element_type=F32) * SCALE
        dkn = dot_first(ds, q) * SCALE
        out[left(1)] = norm_backward(dqn, qhat, qinv).astype(BF16)
        out[right(1)] = norm_backward(dkn, khat, kinv).astype(BF16)
        out[left(2)] = dot_first(half, datt).astype(BF16)


def finish_kernel(
    down, inp, cot, unit, inv, spread, tri, exp, mer, shr, outputs, block_grad, tgrad, egrad, mgrad, sgrad,
    held, slots, acc, xsend, xgot, stat_out, stat_in, ring, left, res, got,
    wsem, zs, zr, ys, yr, cs, cr, xs, xr, ss, sr, ls, lr, gs, gr, osem,
):
    r, m, x, y, z, c = place()
    refs = named(tri, exp, mer, shr)
    grads = named(tgrad, egrad, mgrad, sgrad)
    peers = partners(m, y, z, c)
    xpeers = [(x + i) % 4 for i in (1, 2, 3)]
    inner = m % 8
    up = {"dp": (r + z) % 4, "mx": inner + 8 * (1 - z)}
    below = {"dp": (r + 3 + z) % 4, "mx": inner + 8 * (1 - z)}
    other_core = 1 - 2 * c
    opposite = (m + 4) % 8 + 8 * z
    near = (None, peers[1], peers[0], opposite)

    def mate(dc, ab):
        base = m if ab == 0 else near[ab]
        return {"mx": base + other_core if dc else base}

    mates = [(dc, ab) for ab in (3, 2, 1, 0) for dc in (0, 1) if dc or ab]
    greet([up, below] + [mate(dc, ab) for dc, ab in mates] + [{"my": q} for q in xpeers])

    top, bottom = pl.ds(0, 128), pl.ds(128, 128)

    def hop(p, k, way):
        sem = (zs.at[p, k, way], zr.at[p, k, way])
        if way == 0:
            src = down.at[p] if k == 0 else ring.at[8 - k, p]
            dst = ring.at[7 - k, p]
            if k == 3:
                src, dst = src.at[top], dst.at[top]
            return remote(src, dst, *sem, up)
        src = down.at[p] if k == 0 else ring.at[k, p]
        dst = ring.at[k + 1, p]
        if k == 3:
            src, dst = src.at[bottom], dst.at[bottom]
        return remote(src, dst, *sem, below)

    def hop_start(p, k):
        hop(p, k, 0).start()
        hop(p, k, 1).start()

    def hop_wait(p, k):
        hop(p, k, 0).wait_recv()
        hop(p, k, 1).wait_recv()

    def y_send(dz, k):
        src = down if dz == 0 else ring.at[1 + 6 * z]
        sem = (ys.at[dz, k], yr.at[dz, k])
        if k == 0:
            return remote(src, slots.at[dz, 2, 0], *sem, {"mx": peers[0]})
        if k == 1:
            return remote(src, slots.at[dz, 1, 0], *sem, {"mx": peers[1]})
        if k == 2:
            return remote(slots.at[dz, 2, 0, :, top], slots.at[dz, 3, 0, :, top], *sem, {"mx": peers[1]})
        return remote(slots.at[dz, 1, 0, :, bottom], slots.at[dz, 3, 0, :, bottom], *sem, {"mx": peers[0]})

    def core_send(dz, ab):
        src = slots.at[dz, ab, 0]
        if ab == 0:
            src = down if dz == 0 else ring.at[1 + 6 * z]
        return remote(src, slots.at[dz, ab, 1], cs.at[dz, ab], cr.at[dz, ab], {"mx": peers[3]})

    def left_at(q):
        return left.at[q // 2, 0, :, :, :, lanes(q % 2)]

    def left_send(i):
        return remote(spread, left_at(x), ls.at[i], lr.at[i], {"my": xpeers[i]})

    left_core = remote(left.at[:, 0], left.at[:, 1], ls.at[3], lr.at[3], {"mx": peers[3]})

    for p in range(3):
        hop_start(p, 0)
    y_send(0, 0).start()
    y_send(0, 1).start()
    core_send(0, 0).start()
    for i in range(3):
        left_send(i).start()
    for p in range(3):
        load_weights(p, refs, held, wsem, y, z, c)
    left[x // 2, 0, :, :, :, lanes(x % 2)] = spread[...]
    ring[0] = down[...]
    acc[...] = jnp.zeros_like(acc)

    def multiply(data, dz, ab, dc):
        s = ab * 4 + dz * 2 + dc
        fourth = ((z + dz) % 2) * ((c + dc) % 2)
        acc[0] += dot_last(data[0], held[0, s])
        acc[1] += dot_last(data[1, :, 128:256], held[1, s, :, 128:256]) + dot_last(data[2], held[2, s])
        acc[1 - fourth] += dot_last(data[1, :, 0:128], held[1, s, :, 0:128])

    def use(dz, ab):
        multiply(slots.at[dz, ab, 0], dz, ab, 0)

    def use_other(dz, ab):
        core_send(dz, ab).wait_recv()
        multiply(slots.at[dz, ab, 1], dz, ab, 1)

    def result(dz, p, dc, ab):
        return remote(
            res.at[dz, p, dc, ab], got.at[dz, p, dc, ab], gs.at[dz, p, dc, ab], gr.at[dz, p, dc, ab], mate(dc, ab)
        )

    def weight_part(dz, p):
        fourth = ((z + dz) % 2) * c

        def total(dc, side, columns):
            sum_of = None
            for k in range(4):
                d = (dz * (1 + 6 * z) + 2 * k) % 8
                term = jnp.dot(
                    left[side, dc, k].reshape(384, 256), ring[d, p, :, columns], preferred_element_type=F32
                )
                sum_of = term if sum_of is None else sum_of + term
            return sum_of.astype(BF16).reshape(4, 96, -1)

        for dc in range(2):
            if p == 1:
                res[dz, p, dc, :, :, 0:128] = total(dc, fourth, slice(0, 128))
                res[dz, p, dc, :, :, 128:256] = total(dc, 0, slice(128, 256))
            else:
                res[dz, p, dc] = total(dc, 1 if p == 0 else 0, slice(0, 256))
        got[dz, p, 0, 0] = res[dz, p, 0, 0]
        for dc, ab in mates:
            result(dz, p, dc, ab).start()

    def store_part(dz, p):
        for dc, ab in mates:
            result(dz, p, dc, ab).wait_recv()

        def step(w, carry):
            yo, zo, co = owner_of(y, z, c, (w // 2) % 2, w % 2, dz, w // 4)
            fourth, usual, last = share_columns(yo, zo, co)

            def start(blocks):
                for half in range(2):
                    name, index = blocks[2 * p + half]
                    pltpu.make_async_copy(
                        got.at[dz, p, w // 4, w % 4, :, pl.ds(128 * half, 128)], grads[name].at[:, lanes(index)], osem
                    ).start()

            @pl.when(fourth)
            def _():
                start(last)

            @pl.when(jnp.logical_not(fourth))
            def _():
                start(usual)

            return carry

        lax.fori_loop(0, 8, step, 0)

    def x_send(i):
        rows_of = pl.ds(pl.multiple_of(xpeers[i] * 64, 64), 64)
        return remote(xsend.at[:, rows_of], xgot.at[i], xs.at[i], xr.at[i], {"my": xpeers[i]})

    for p in range(3):
        wait_weights(p, held, wsem)
    multiply(down, 0, 0, 0)
    hop_wait(0, 0)
    hop_start(0, 1)
    hop_wait(1, 0)
    hop_start(1, 1)
    hop_wait(2, 0)
    y_send(1, 0).start()
    y_send(1, 1).start()
    core_send(1, 0).start()
    y_send(0, 0).wait_recv()
    y_send(0, 2).start()
    core_send(0, 2).start()
    y_send(0, 1).wait_recv()
    y_send(0, 3).start()
    core_send(0, 1).start()
    use_other(0, 0)
    multiply(ring.at[1 + 6 * z], 1, 0, 0)
    hop_wait(0, 1)
    hop_start(0, 2)
    hop_wait(1, 1)
    hop_start(1, 2)
    use(0, 2)
    use(0, 1)
    use_other(1, 0)
    hop_wait(0, 2)
    hop_start(0, 3)
    hop_wait(1, 2)
    hop_start(1, 3)
    hop_start(2, 1)
    y_send(0, 2).wait_recv()
    y_send(0, 3).wait_recv()
    core_send(0, 3).start()
    y_send(1, 0).wait_recv()
    y_send(1, 2).start()
    core_send(1, 2).start()
    y_send(1, 1).wait_recv()
    y_send(1, 3).start()
    core_send(1, 1).start()
    for i in range(3):
        rows_of = left_at((x + 3 - i) % 4)
        remote(spread, rows_of, ls.at[i], lr.at[i], {"my": xpeers[i]}).wait_recv()
    left_core.start()
    use(0, 3)
    use_other(0, 2)
    use_other(0, 1)
    hop_wait(2, 1)
    hop_start(2, 2)
    hop_wait(0, 3)
    left_core.wait_recv()
    weight_part(0, 0)
    weight_part(1, 0)
    hop_wait(1, 3)
    hop_wait(2, 2)
    hop_start(2, 3)
    weight_part(0, 1)
    weight_part(1, 1)
    y_send(1, 2).wait_recv()
    y_send(1, 3).wait_recv()
    core_send(1, 3).start()
    use(1, 2)
    use(1, 1)
    use(1, 3)
    use_other(0, 3)
    for ab in (2, 1, 3):
        use_other(1, ab)

    xsend[...] = acc[...].astype(BF16)
    for i in range(3):
        x_send(i).start()
    hop_wait(2, 3)
    weight_part(0, 2)
    weight_part(1, 2)
    own = pl.ds(pl.multiple_of(x * 64, 64), 64)
    branch = acc[0, own, :]
    grad = acc[1, own, :]
    for i in range(3):
        x_send(i).wait_recv()
        branch = branch + xgot[i, 0].astype(F32)
        grad = grad + xgot[i, 1].astype(F32)
    outputs[...] = (inp[...].astype(F32) + branch).astype(BF16)
    hat = unit[...]
    first = jnp.sum(grad, axis=1, keepdims=True)
    second = jnp.sum(grad * hat, axis=1, keepdims=True)
    low = lax.broadcasted_iota(jnp.int32, (64, 128), 1) < 64
    parts = [(dz, p) for p in range(3) for dz in range(2)]
    for step in range(4):
        stat_out[step] = jnp.where(low, first, second)
        copy = remote(
            stat_out.at[step], stat_in.at[step], ss.at[step], sr.at[step], {"mx": peers[(3, 0, 1, 2)[step]]}
        )
        copy.start()
        if step < 3:
            store_part(*parts[step])
        copy.wait()
        other = stat_in[step]
        first = first + other[:, 0:1]
        second = second + other[:, 64:65]
    fixed = (grad - first / WIDTH - hat * (second / WIDTH)) * inv[:, 0:1]
    block_grad[...] = (cot[...].astype(F32) + fixed).astype(BF16)
    for dz, p in parts[3:]:
        store_part(dz, p)

    for p in range(3):
        for k in range(4):
            for way in range(2):
                hop(p, k, way).wait_send()
    for dz in range(2):
        for k in range(4):
            y_send(dz, k).wait_send()
            core_send(dz, k).wait_send()
    for i in range(3):
        x_send(i).wait_send()
        left_send(i).wait_send()
    left_core.wait_send()
    for dz, p in parts:
        for dc, ab in mates:
            result(dz, p, dc, ab).wait_send()
    pltpu.make_async_copy(got, got, osem).wait()


def params(number=None):
    if number is None:
        return pltpu.CompilerParams(vmem_limit_bytes=VMEM_LIMIT)
    return pltpu.CompilerParams(collective_id=number, has_side_effects=True, vmem_limit_bytes=VMEM_LIMIT)


VM = pl.BlockSpec(memory_space=pltpu.VMEM)
HB = pl.BlockSpec(memory_space=pl.ANY)
SEM = pltpu.SemaphoreType.DMA


def shape(*dims, dtype=BF16):
    return jax.ShapeDtypeStruct(dims, dtype)


def project(inp, cot, tri, exp, mer, shr):
    return pl.pallas_call(
        project_kernel,
        out_shape=(
            shape(3, 256, 256, dtype=F32), shape(64, 384, dtype=F32), shape(64, 128, dtype=F32), shape(4, 4, 96, 128),
        ),
        in_specs=[VM, VM, HB, HB, HB, HB],
        out_specs=(VM,) * 4,
        scratch_shapes=[
            pltpu.VMEM((3, 16, 384, 256), BF16),
            pltpu.VMEM((3, 3, 2, 8, 96, 256), BF16),
            pltpu.VMEM((3, 3, 8, 96, 256), BF16),
            pltpu.VMEM((3, 3, 4, 96, 256), BF16),
            pltpu.VMEM((3, 3, 2, 96, 256), BF16),
            pltpu.VMEM((3, 3, 1, 96, 256), BF16),
            pltpu.VMEM((4, 64, 128), F32),
            pltpu.VMEM((4, 64, 128), F32),
            pltpu.VMEM((64, 384), BF16),
            pltpu.VMEM((2, 256, 384), BF16),
            pltpu.VMEM((4, 96, 128), BF16),
            pltpu.VMEM((4, 96, 128), BF16),
            SEM((3,)), SEM((2, 3)), SEM((2, 3)), SEM((4,)), SEM((4,)), SEM((3, 3, 4)), SEM((3, 3, 4)),
            SEM((3,)), SEM((3,)), SEM((4,)), SEM((4,)),
        ],
        compiler_params=params(0),
        name="project",
    )(inp, cot, tri, exp, mer, shr)


def middle(proj):
    return pl.pallas_call(
        middle_kernel,
        out_shape=shape(3, 256, 256),
        in_specs=[VM],
        out_specs=VM,
        compiler_params=params(),
        name="middle",
    )(proj)


def finish(down, inp, cot, unit, inv, spread, tri, exp, mer, shr):
    return pl.pallas_call(
        finish_kernel,
        out_shape=(
            shape(64, 384), shape(64, 384), shape(3, 96, 1536), shape(96, 3072), shape(96, 1536), shape(96, 3072),
        ),
        in_specs=[VM] * 6 + [HB] * 4,
        out_specs=(VM, VM) + (HB,) * 4,
        scratch_shapes=[
            pltpu.VMEM((3, 16, 384, 256), BF16),
            pltpu.VMEM((2, 4, 2, 3, 256, 256), BF16),
            pltpu.VMEM((2, 256, 384), F32),
            pltpu.VMEM((2, 256, 384), BF16),
            pltpu.VMEM((3, 2, 64, 384), BF16),
            pltpu.VMEM((4, 64, 128), F32),
            pltpu.VMEM((4, 64, 128), F32),
            pltpu.VMEM((8, 3, 256, 256), BF16),
            pltpu.VMEM((2, 2, 4, 4, 96, 256), BF16),
            pltpu.VMEM((2, 3, 2, 4, 96, 256), BF16),
            pltpu.VMEM((2, 3, 2, 4, 96, 256), BF16),
            SEM((3,)), SEM((3, 4, 2)), SEM((3, 4, 2)), SEM((2, 4)), SEM((2, 4)), SEM((2, 4)), SEM((2, 4)),
            SEM((3,)), SEM((3,)), SEM((4,)), SEM((4,)), SEM((4,)), SEM((4,)),
            SEM((2, 3, 2, 4)), SEM((2, 3, 2, 4)), SEM(()),
        ],
        compiler_params=params(1),
        name="finish",
    )(down, inp, cot, unit, inv, spread, tri, exp, mer, shr)


def body(inputs, triple_weight, expand_weight, merge_weight, shrink_weight, cotangent):
    weights = (triple_weight.transpose(1, 0, 2), expand_weight, merge_weight, shrink_weight)
    proj, unit, inv, spread = project(inputs, cotangent, *weights)
    down = middle(proj)
    outputs, block_grad, tg, eg, mg, sg = finish(down, inputs, cotangent, unit, inv, spread, *weights)
    return outputs, block_grad, tg.transpose(1, 0, 2), eg, mg, sg


def solution(mesh):
    placed = (
        P(("dp", "my"), "mx"),
        P("mx", None, "my"),
        P("mx", "my"),
        P("mx", "my"),
        P("mx", "my"),
        P(("dp", "my"), "mx"),
    )
    return jax.shard_map(
        body,
        mesh=mesh,
        in_specs=placed,
        out_specs=(
            P(("dp", "my"), "mx"),
            P(("dp", "my"), "mx"),
            P(("mx", "dp"), None, "my"),
            P(("mx", "dp"), "my"),
            P(("mx", "dp"), "my"),
            P(("mx", "dp"), "my"),
        ),
        check_vma=False,
    )
```

time: 224 us -> 139 us (0.62)
  Pallas kernels: 164 us -> 129 us
  blocking collectives: 27.8 us -> 0 us
  between operations: 14.1 us -> 0.68 us
  local copies, waits for them, and re-layouts: 16.6 us -> 7.44 us
    pallas_call x2 -> x1, Pallas kernels: 105 us -> 70.7 us  [finish(): pl.pallas_call(finish_kernel, out_shape=(shape(64, 384), shape(64, 384),...]
    all_gather x2 -> x0, blocking collectives: 27.8 us -> none  [the longest x1 17.5 us: row_shares(): all_reps = lax.all_gather(pair, 'dp')]
    reshape x2 -> x0, local copies, waits for them, and re-layouts: 6.04 us -> none  [the longest x1 3.8 us: body(): tri = triple_weight.reshape(triple_weight.shape[0], -1)]
    unnamed x17 -> x12, local copies, waits for them, and re-layouts: 9.35 us -> 7.44 us
  transfers between devices with their start and end apart: 1 -> 0, of which waited for: 0 -> 0; matrix products, arithmetic and copies ran while one was open for 0% -> 0% of each run, Pallas kernels for 32% -> 0%
where the time goes in v2:
time: 139 us; the launch traced here: 137 us
  Pallas kernels  129 us (93%)
  local copies, waits for them, and re-layouts  7.44 us (5%)
    pallas_call x1, Pallas kernels, finish(): pl.pallas_call(finish_kernel, out_shape=(shape(64, 384), shape(64, 384),...  70.7 us
    pallas_call x1, Pallas kernels, project(): pl.pallas_call(project_kernel, out_shape=(shape(3, 256, 256, dtype=F32),...  55.4 us
    unnamed x12, local copies, waits for them, and re-layouts  7.44 us
    pallas_call x1, Pallas kernels, middle(): pl.pallas_call(middle_kernel, out_shape=shape(3, 256, 256), in_specs=[VM]...  3.16 us

profile of v2, /device:TPU:1, one launch (start us, length us, event | category | flops | bytes accessed | tf_op | source)
XLA Modules:
  0.0 137.4 jit_solution(16983075350605872479)
XLA Ops:
  0.6 55.4 %project.1 = (f32[3,256,256]{2,1,0:T(8,128)}, f32[64,384]{1,0:T(8,128)}, f32[64,128]{1,0:T(8,128)}, bf16[4,4,96,128]{3,2,1,0:T(8,128)(2,1)}) custom-call(bf16[64,384]{1,0:T(8,128)(2,1)} %inp.3, bf16[64,384]{1,0:T(8,128)(2,1)} %cot.3, bf16[3,384,1536]{2,1,0:T(8,128)(2,1)} %bitcast.2, bf16[384,3072]{1,0:T(8,128)(2,1)} %exp.3, bf16[384,1536]{1,0:T(8,128)(2,1)} %mer.3, ...), custom_call_target="tpu_custom_call" | custom-call | tf_op jit(solution)/shard_map/project/pallas_call | solution.py:671
  56.1 3.2 %middle.1.down = bf16[3,256,256]{2,1,0:T(8,128)(2,1)} custom-call(f32[3,256,256]{2,1,0:T(8,128)} %get-tuple-element.16.proj), custom_call_target="tpu_custom_call" | custom-call | tf_op jit(solution)/shard_map/middle/pallas_call | solution.py:700
  59.2 70.7 %finish.1 = (bf16[64,384]{1,0:T(8,128)(2,1)}, bf16[64,384]{1,0:T(8,128)(2,1)}, bf16[3,96,1536]{2,1,0:T(8,128)(2,1)}, bf16[96,3072]{1,0:T(8,128)(2,1)}, bf16[96,1...) custom-call(bf16[3,256,256]{2,1,0:T(8,128)(2,1)} %middle.1.down, bf16[64,384]{1,0:T(8,128)(2,1)} %inp.3, bf16[64,384]{1,0:T(8,128)(2,1)} %cot.3, ...), custom_call_target="tpu_custom_call" | custom-call | tf_op jit(solution)/shard_map/finish/pallas_call | solution.py:711
  129.9 0.0 copy-start.1
  129.9 0.0 copy-start.2
  130.0 0.0 copy-start
  130.0 1.5 %copy.18 = bf16[64,384]{1,0:T(8,128)(2,1)} copy(bf16[64,384]{1,0:T(8,128)(2,1)} %get-tuple-element.32) | data formatting | bytes 98304
  131.5 1.4 %copy.19 = bf16[64,384]{1,0:T(8,128)(2,1)} copy(bf16[64,384]{1,0:T(8,128)(2,1)} %get-tuple-element.33) | data formatting | bytes 98304
  132.9 2.1 %copy.20 = bf16[96,3,1536]{2,0,1:T(8,128)(2,1)} copy(bf16[96,3,1536]{2,0,1:T(8,128)(2,1)} %bitcast.4) | data formatting | bytes 1769472
  135.1 0.0 copy-done.1
  135.1 0.8 copy.21
  135.9 0.0 copy-done.2
  135.9 0.7 copy.22
  136.6 0.0 copy-done
  136.6 0.8 copy.23
Async XLA Ops:
  129.9 5.1 %copy-start.1 = (bf16[96,3072]{1,0:T(8,128)(2,1)S(1)}, bf16[96,3072]{1,0:T(8,128)(2,1)}, u32[]{:S(2)}) copy-start(bf16[96,3072]{1,0:T(8,128)(2,1)} %get-tuple-element.35) | copy-start | bytes 1769476
  129.9 5.9 %copy-start.2 = (bf16[96,1536]{1,0:T(8,128)(2,1)S(1)}, bf16[96,1536]{1,0:T(8,128)(2,1)}, u32[]{:S(2)}) copy-start(bf16[96,1536]{1,0:T(8,128)(2,1)} %get-tuple-element.36) | copy-start | bytes 884740
  130.0 6.6 %copy-start = (bf16[96,3072]{1,0:T(8,128)(2,1)S(1)}, bf16[96,3072]{1,0:T(8,128)(2,1)}, u32[]{:S(2)}) copy-start(bf16[96,3072]{1,0:T(8,128)(2,1)} %get-tuple-element.37) | copy-start | bytes 1769476

commit v3 on v2

v3 whole, which is shorter than its diff:
```python
import math

import jax
import jax.numpy as jnp
from jax import lax
from jax.experimental import pallas as pl
from jax.experimental.pallas import tpu as pltpu
from jax.sharding import PartitionSpec as P

MESH = pl.DeviceIdType.MESH
F32 = jnp.float32
BF16 = jnp.bfloat16

WIDTH = 6144
EPS = 1e-06
ROOT_HALF = 0.7071067811865476
INV_ROOT_TAU = 0.3989422804014327
SCALE = 1.0 / math.sqrt(128)
VMEM_LIMIT = 60 * 1024 * 1024

SEQ = ((0, 1, 2), (1, 2, 0), (2, 0, 1))
CUTS = (((0, 96), (96, 80), (176, 80)), ((0, 80), (80, 96), (176, 80)), ((0, 80), (80, 80), (160, 96)))


def place():
    m = lax.axis_index("mx")
    c = m % 2
    y = (m // 2) % 4
    z = m // 8
    return lax.axis_index("dp"), m, lax.axis_index("my"), y, z, c


def partners(m, y, z, c):
    return (m + 2 * (1 - 2 * (y % 2)), m + 2 * (3 - 2 * y), m + 8 - 16 * z, m + 1 - 2 * c)


def owner_of(y, z, c, da, db, dz, dc):
    b = (y // 2 + db) % 2
    a = (y + y // 2 + da) % 2
    return 2 * b + (a + b) % 2, (z + dz) % 2, (c + dc) % 2


def share_columns(yo, zo, co):
    k = zo * 2 + co
    head = 3 * yo + k
    unit = 6 * yo + k
    usual = (("m", head), ("s", unit), ("q", head), ("k", head), ("v", head), ("e", unit))
    first = 6 * yo + 3
    fourth = (("s", first), ("s", first + 1), ("s", first + 2), ("e", first), ("e", first + 1), ("e", first + 2))
    return k == 3, usual, fourth


def named(tri, exp, mer, shr):
    return {"q": tri.at[0], "k": tri.at[1], "v": tri.at[2], "e": exp, "m": mer, "s": shr}


def lanes(index):
    return pl.ds(pl.multiple_of(index * 128, 128), 128)


def load_weights(p, refs, held, sem, y, z, c):
    def step(s, carry):
        yo, zo, co = owner_of(y, z, c, s // 8, (s // 4) % 2, (s // 2) % 2, s % 2)
        fourth, usual, last = share_columns(yo, zo, co)

        def start(blocks):
            for half in range(2):
                name, index = blocks[2 * p + half]
                pltpu.make_async_copy(
                    refs[name].at[:, lanes(index)], held.at[p, s, :, pl.ds(128 * half, 128)], sem.at[p]
                ).start()

        @pl.when(fourth)
        def _():
            start(last)

        @pl.when(jnp.logical_not(fourth))
        def _():
            start(usual)

        return carry

    lax.fori_loop(0, 16, step, 0)


def wait_weights(p, held, sem):
    pltpu.make_async_copy(held.at[p], held.at[p], sem.at[p]).wait()


def remote(src, dst, send, recv, device):
    return pltpu.make_async_remote_copy(
        src_ref=src, dst_ref=dst, send_sem=send, recv_sem=recv, device_id=device, device_id_type=MESH
    )


def greet(devices):
    barrier = pltpu.get_barrier_semaphore()
    for device in devices:
        pl.semaphore_signal(barrier, inc=1, device_id=device, device_id_type=MESH)
    pl.semaphore_wait(barrier, len(devices))


def dot_last(left, right):
    return lax.dot_general(left, right, (((1,), (1,)), ((), ())), preferred_element_type=F32)


def dot_first(left, right):
    return lax.dot_general(left, right, (((0,), (0,)), ((), ())), preferred_element_type=F32)


def norm_heads(block):
    centre = block - jnp.mean(block, axis=-1, keepdims=True)
    inverse = lax.rsqrt(jnp.mean(centre * centre, axis=-1, keepdims=True) + EPS)
    return centre * inverse, inverse


def norm_backward(grad, unit, inverse):
    first = jnp.mean(grad, axis=-1, keepdims=True)
    second = jnp.mean(grad * unit, axis=-1, keepdims=True)
    return (grad - first - unit * second) * inverse


def gelu_pair(pre):
    phi = 0.5 * (1.0 + lax.erf(pre * ROOT_HALF))
    return pre * phi, phi + pre * jnp.exp(-0.5 * pre * pre) * INV_ROOT_TAU


def middle(proj, out, fourth):
    def left(p):
        return (p, slice(None), slice(0, 128))

    def right(p):
        return (p, slice(None), slice(128, 256))

    def unit(pre_at, grad_at):
        value, slope = gelu_pair(proj[pre_at])
        grad = proj[grad_at]
        out[grad_at] = value.astype(BF16)
        out[pre_at] = (grad * slope).astype(BF16)

    @pl.when(fourth)
    def _():
        unit(right(1), left(0))
        unit(left(2), right(0))
        unit(right(2), left(1))

    @pl.when(jnp.logical_not(fourth))
    def _():
        unit(right(2), right(0))
        qhat, qinv = norm_heads(proj[left(1)])
        khat, kinv = norm_heads(proj[right(1)])
        q, k = qhat.astype(BF16), khat.astype(BF16)
        v = proj[left(2)].astype(BF16)
        datt = proj[left(0)].astype(BF16)
        expo = jnp.exp(dot_last(q, k) * SCALE)
        probs = expo / jnp.sum(expo, axis=-1, keepdims=True)
        half = probs.astype(BF16)
        out[left(0)] = jnp.dot(half, v, preferred_element_type=F32).astype(BF16)
        g = dot_last(datt, v)
        ds = (probs * (g - jnp.sum(probs * g, axis=-1, keepdims=True))).astype(BF16)
        dqn = jnp.dot(ds, k, preferred_element_type=F32) * SCALE
        dkn = dot_first(ds, q) * SCALE
        out[left(1)] = norm_backward(dqn, qhat, qinv).astype(BF16)
        out[right(1)] = norm_backward(dkn, khat, kinv).astype(BF16)
        out[left(2)] = dot_first(half, datt).astype(BF16)


def block_kernel(
    inp, cot, tri, exp, mer, shr, outputs, block_grad, got,
    held, part, got0, got1, got2, got3, stat_out, stat_in, nown, both, turned, mixed, spread, hat, proj, down,
    slots, acc, xsend, xgot, ring, left, res,
    wsem, xs, xr, ss, sr, rs, rr, es, er, fs, fr, zs, zr, ys, yr, cs, cr, ls, lr, gs, gr, osem,
):
    r, m, x, y, z, c = place()
    refs = named(tri, exp, mer, shr)
    peers = partners(m, y, z, c)
    xpeers = [(x + i) % 4 for i in (1, 2, 3)]
    rpeers = [(r + i) % 4 for i in (1, 2, 3)]
    inner = m % 8
    up = {"dp": (r + z) % 4, "mx": inner + 8 * (1 - z)}
    below = {"dp": (r + 3 + z) % 4, "mx": inner + 8 * (1 - z)}
    other_core = 1 - 2 * c
    opposite = (m + 4) % 8 + 8 * z
    near = (None, peers[1], peers[0], opposite)

    def mate(dc, ab):
        base = m if ab == 0 else near[ab]
        return {"mx": base + other_core if dc else base}

    mates = [(dc, ab) for ab in (3, 2, 1, 0) for dc in (0, 1) if dc or ab]
    rounds = (
        ({"mx": peers[3]}, {"mx": peers[2]}, {"mx": peers[2] + other_core}),
        ({"mx": peers[0]}, {"mx": peers[1]}, {"mx": opposite}),
    )
    greet(
        [{"my": q} for q in xpeers] + [{"dp": q} for q in rpeers] + [up, below, rounds[0][2]]
        + [mate(dc, ab) for dc, ab in mates]
    )

    own = pl.ds(pl.multiple_of(x * 64, 64), 64)
    sends = []
    for i in range(3):
        copy = remote(cot, both.at[1, own], xs.at[0, i], xr.at[0, i], {"my": xpeers[i]})
        copy.start()
        sends.append(copy)
    both[1, own, :] = cot[...]

    rows = inp[...].astype(F32)
    mean = jnp.sum(rows, axis=1, keepdims=True) / rows.shape[1]
    centred = rows - mean
    square = jnp.sum(centred * centred, axis=1, keepdims=True)
    low = lax.broadcasted_iota(jnp.int32, (64, 128), 1) < 64

    def stat_copy(k, i):
        return remote(stat_out.at[k], stat_in.at[k, i], ss.at[k, i], sr.at[k, i], rounds[k % 2][i])

    def stat_start(k, pair):
        stat_out[k] = jnp.where(low, pair[0], pair[1])
        for i in range(3):
            stat_copy(k, i).start()

    def stat_finish(k):
        pairs = []
        for i in range(3):
            stat_copy(k, i).wait_recv()
            pairs.append((stat_in[k, i, :, 0:1], stat_in[k, i, :, 64:65]))
        return pairs

    def combine(own_pair, pairs, count):
        pairs = [own_pair] + pairs
        middle_of = sum(pair[0] for pair in pairs) / 4
        spread_of = sum(pair[1] + count * (pair[0] - middle_of) ** 2 for pair in pairs)
        return middle_of, spread_of

    pair = (mean, square)
    stat_start(0, pair)
    load_weights(0, refs, held, wsem, y, z, c)
    pair = combine(pair, stat_finish(0), 384.0)
    stat_start(1, pair)

    def gathered(k):
        for i in range(3):
            rows_of = both.at[1 - k, pl.ds(pl.multiple_of(((x + 3 - i) % 4) * 64, 64), 64)]
            remote(rows_of, rows_of, xs.at[k, i], xr.at[k, i], {"my": xpeers[i]}).wait_recv()

    def multiply(p, dc):
        def step(t, carry):
            da, db, dz = t // 4, (t // 2) % 2, t % 2
            s = t * 2 + dc
            places = (t, 4 * db + 2 * dz + da, 4 * dz + 2 * da + db)

            def put(value, columns):
                for q in range(3):
                    at, size = CUTS[p][q]
                    part[p, q, dc, places[q], 0:size, columns] = value[at : at + size]

            if p == 1:
                fourth = ((z + dz) % 2) * ((c + dc) % 2)
                first = jnp.dot(both[fourth], held[p, s, :, 0:128], preferred_element_type=F32)
                second = jnp.dot(both[0], held[p, s, :, 128:256], preferred_element_type=F32)
                put(first.astype(BF16), slice(0, 128))
                put(second.astype(BF16), slice(128, 256))
            else:
                full = both[1 if p == 0 else 0]
                put(jnp.dot(full, held[p, s], preferred_element_type=F32).astype(BF16), slice(0, 256))
            return carry

        lax.fori_loop(0, 8, step, 0)

    def stage(p, q, k):
        size = CUTS[p][q][1]
        sem = (rs.at[p, q, k], rr.at[p, q, k])
        if k == 0:
            return remote(part.at[p, q, 1, :, 0:size], got0.at[p, q, :, 0:size], *sem, {"mx": peers[3]})
        slots = 8 >> k
        target = (None, got1, got2, got3)[k]
        return remote(
            part.at[p, q, 0, pl.ds(slots, slots), 0:size], target.at[p, q, :, 0:size], *sem,
            {"mx": peers[SEQ[q][k - 1]]},
        )

    def begin(p):
        for q in range(3):
            stage(p, q, 0).start()

    def advance(p, k):
        source = (got0, got1, got2, got3)[k]
        for q in range(3):
            at, size = CUTS[p][q]
            stage(p, q, k).wait_recv()

            def step(t, carry):
                total = part[p, q, 0, t, 0:size].astype(F32) + source[p, q, t, 0:size].astype(F32)
                part[p, q, 0, t, 0:size] = total.astype(BF16)
                return carry

            if k < 3:
                lax.fori_loop(0, 8 >> k, step, 0)
                stage(p, q, k + 1).start()
            else:
                proj[p, at : at + size] = (
                    part[p, q, 0, 0, 0:size].astype(F32) + source[p, q, 0, 0:size].astype(F32)
                )

    def swap(i):
        q = rpeers[i]
        return remote(turned.at[q], mixed.at[3 - i], es.at[i], er.at[i], {"dp": q})

    def pass_on(k):
        sem = (fs.at[k], fr.at[k])
        if k == 0:
            return remote(mixed, spread.at[:, 2], *sem, {"mx": peers[0]})
        if k == 1:
            return remote(mixed, spread.at[:, 1], *sem, {"mx": peers[1]})
        if k == 2:
            return remote(spread.at[0:2, 2], spread.at[0:2, 3], *sem, {"mx": peers[1]})
        return remote(spread.at[2:4, 1], spread.at[2:4, 3], *sem, {"mx": peers[0]})

    gathered(0)
    wait_weights(0, held, wsem)
    multiply(0, 1)
    begin(0)
    pair = combine(pair, stat_finish(1), 1536.0)
    inverse = lax.rsqrt(pair[1] / WIDTH + EPS)
    unit = (rows - pair[0]) * inverse
    nown[...] = unit.astype(BF16)
    both[0, own, :] = unit.astype(BF16)
    for i in range(3):
        copy = remote(nown, both.at[0, own], xs.at[1, i], xr.at[1, i], {"my": xpeers[i]})
        copy.start()
        sends.append(copy)
    hat[...] = unit
    multiply(0, 0)
    load_weights(1, refs, held, wsem, y, z, c)
    advance(0, 0)
    load_weights(2, refs, held, wsem, y, z, c)
    advance(0, 1)
    gathered(1)
    wait_weights(1, held, wsem)
    multiply(1, 1)
    begin(1)
    multiply(1, 0)
    wait_weights(2, held, wsem)
    multiply(2, 1)
    begin(2)
    advance(1, 0)

    quarter = both[x // 2, pl.ds(pl.multiple_of((x % 2) * 128, 128), 128), :]
    turned[...] = quarter.T.reshape(4, 96, 128)
    for i in range(3):
        swap(i).start()
    mixed[0] = turned[r]
    multiply(2, 0)
    advance(2, 0)
    advance(0, 2)
    advance(1, 1)
    advance(2, 1)
    for i in range(3):
        swap(i).wait_recv()
    pass_on(0).start()
    pass_on(1).start()
    spread[:, 0] = mixed[...]
    advance(1, 2)
    advance(2, 2)
    pass_on(0).wait_recv()
    pass_on(2).start()
    pass_on(1).wait_recv()
    pass_on(3).start()
    for p in range(3):
        advance(p, 3)
    middle(proj, down, z * 2 + c == 3)

    top, bottom = pl.ds(0, 128), pl.ds(128, 128)

    def hop(p, k, way):
        sem = (zs.at[p, k, way], zr.at[p, k, way])
        if way == 0:
            src = down.at[p] if k == 0 else ring.at[8 - k, p]
            dst = ring.at[7 - k, p]
            if k == 3:
                src, dst = src.at[top], dst.at[top]
            return remote(src, dst, *sem, up)
        src = down.at[p] if k == 0 else ring.at[k, p]
        dst = ring.at[k + 1, p]
        if k == 3:
            src, dst = src.at[bottom], dst.at[bottom]
        return remote(src, dst, *sem, below)

    def hop_start(p, k):
        hop(p, k, 0).start()
        hop(p, k, 1).start()

    def hop_wait(p, k):
        hop(p, k, 0).wait_recv()
        hop(p, k, 1).wait_recv()

    def y_send(dz, k):
        src = down if dz == 0 else ring.at[1 + 6 * z]
        sem = (ys.at[dz, k], yr.at[dz, k])
        if k == 0:
            return remote(src, slots.at[dz, 2, 0], *sem, {"mx": peers[0]})
        if k == 1:
            return remote(src, slots.at[dz, 1, 0], *sem, {"mx": peers[1]})
        if k == 2:
            return remote(slots.at[dz, 2, 0, :, top], slots.at[dz, 3, 0, :, top], *sem, {"mx": peers[1]})
        return remote(slots.at[dz, 1, 0, :, bottom], slots.at[dz, 3, 0, :, bottom], *sem, {"mx": peers[0]})

    def core_send(dz, ab):
        src = slots.at[dz, ab, 0]
        if ab == 0:
            src = down if dz == 0 else ring.at[1 + 6 * z]
        return remote(src, slots.at[dz, ab, 1], cs.at[dz, ab], cr.at[dz, ab], {"mx": peers[3]})

    def left_at(q):
        return left.at[q // 2, 0, :, :, :, lanes(q % 2)]

    def left_send(i):
        return remote(spread, left_at(x), ls.at[i], lr.at[i], {"my": xpeers[i]})

    left_core = remote(left.at[:, 0], left.at[:, 1], ls.at[3], lr.at[3], {"mx": peers[3]})

    for p in range(3):
        hop_start(p, 0)
    y_send(0, 0).start()
    y_send(0, 1).start()
    core_send(0, 0).start()
    pass_on(2).wait_recv()
    pass_on(3).wait_recv()
    for i in range(3):
        left_send(i).start()
    left[x // 2, 0, :, :, :, lanes(x % 2)] = spread[...]
    ring[0] = down[...]
    acc[...] = jnp.zeros_like(acc)

    def dgrad(data, dz, ab, dc):
        s = ab * 4 + dz * 2 + dc
        fourth = ((z + dz) % 2) * ((c + dc) % 2)
        acc[0] += dot_last(data[0], held[0, s])
        acc[1] += dot_last(data[1, :, 128:256], held[1, s, :, 128:256]) + dot_last(data[2], held[2, s])
        acc[1 - fourth] += dot_last(data[1, :, 0:128], held[1, s, :, 0:128])

    def use(dz, ab):
        dgrad(slots.at[dz, ab, 0], dz, ab, 0)

    def use_other(dz, ab):
        core_send(dz, ab).wait_recv()
        dgrad(slots.at[dz, ab, 1], dz, ab, 1)

    def result(dz, p, dc, ab):
        return remote(
            res.at[dz, p, dc, ab], got.at[dz, p, dc, ab], gs.at[dz, p, dc, ab], gr.at[dz, p, dc, ab], mate(dc, ab)
        )

    def weight_part(dz, p):
        fourth = ((z + dz) % 2) * c

        def total(dc, side, columns):
            sum_of = None
            for k in range(4):
                d = (dz * (1 + 6 * z) + 2 * k) % 8
                term = jnp.dot(
                    left[side, dc, k].reshape(384, 256), ring[d, p, :, columns], preferred_element_type=F32
                )
                sum_of = term if sum_of is None else sum_of + term
            return sum_of.astype(BF16).reshape(4, 96, -1)

        for dc in range(2):
            if p == 1:
                res[dz, p, dc, :, :, 0:128] = total(dc, fourth, slice(0, 128))
                res[dz, p, dc, :, :, 128:256] = total(dc, 0, slice(128, 256))
            else:
                res[dz, p, dc] = total(dc, 1 if p == 0 else 0, slice(0, 256))
        pltpu.make_async_copy(res.at[dz, p, 0, 0], got.at[dz, p, 0, 0], osem).start()
        for dc, ab in mates:
            result(dz, p, dc, ab).start()

    def x_send(i):
        rows_of = pl.ds(pl.multiple_of(xpeers[i] * 64, 64), 64)
        return remote(xsend.at[:, rows_of], xgot.at[i], xs.at[2, i], xr.at[2, i], {"my": xpeers[i]})

    dgrad(down, 0, 0, 0)
    hop_wait(0, 0)
    hop_start(0, 1)
    hop_wait(1, 0)
    hop_start(1, 1)
    hop_wait(2, 0)
    y_send(1, 0).start()
    y_send(1, 1).start()
    core_send(1, 0).start()
    y_send(0, 0).wait_recv()
    y_send(0, 2).start()
    core_send(0, 2).start()
    y_send(0, 1).wait_recv()
    y_send(0, 3).start()
    core_send(0, 1).start()
    use_other(0, 0)
    dgrad(ring.at[1 + 6 * z], 1, 0, 0)
    hop_wait(0, 1)
    hop_start(0, 2)
    hop_wait(1, 1)
    hop_start(1, 2)
    use(0, 2)
    use(0, 1)
    use_other(1, 0)
    hop_wait(0, 2)
    hop_start(0, 3)
    hop_wait(1, 2)
    hop_start(1, 3)
    hop_start(2, 1)
    y_send(0, 2).wait_recv()
    y_send(0, 3).wait_recv()
    core_send(0, 3).start()
    y_send(1, 0).wait_recv()
    y_send(1, 2).start()
    core_send(1, 2).start()
    y_send(1, 1).wait_recv()
    y_send(1, 3).start()
    core_send(1, 1).start()
    for i in range(3):
        rows_of = left_at((x + 3 - i) % 4)
        remote(spread, rows_of, ls.at[i], lr.at[i], {"my": xpeers[i]}).wait_recv()
    left_core.start()
    use(0, 3)
    use_other(0, 2)
    use_other(0, 1)
    hop_wait(2, 1)
    hop_start(2, 2)
    hop_wait(0, 3)
    left_core.wait_recv()
    weight_part(0, 0)
    weight_part(1, 0)
    hop_wait(1, 3)
    hop_wait(2, 2)
    hop_start(2, 3)
    weight_part(0, 1)
    weight_part(1, 1)
    y_send(1, 2).wait_recv()
    y_send(1, 3).wait_recv()
    core_send(1, 3).start()
    use(1, 2)
    use(1, 1)
    use(1, 3)
    use_other(0, 3)
    for ab in (2, 1, 3):
        use_other(1, ab)

    xsend[...] = acc[...].astype(BF16)
    for i in range(3):
        x_send(i).start()
    hop_wait(2, 3)
    weight_part(0, 2)
    weight_part(1, 2)
    own = pl.ds(pl.multiple_of(x * 64, 64), 64)
    branch = acc[0, own, :]
    grad = acc[1, own, :]
    for i in range(3):
        x_send(i).wait_recv()
        branch = branch + xgot[i, 0].astype(F32)
        grad = grad + xgot[i, 1].astype(F32)
    outputs[...] = (inp[...].astype(F32) + branch).astype(BF16)
    unit = hat[...]
    sums = (jnp.sum(grad, axis=1, keepdims=True), jnp.sum(grad * unit, axis=1, keepdims=True))
    for k in (2, 3):
        stat_start(k, sums)
        for pair in stat_finish(k):
            sums = (sums[0] + pair[0], sums[1] + pair[1])
    fixed = (grad - sums[0] / WIDTH - unit * (sums[1] / WIDTH)) * inverse
    block_grad[...] = (cot[...].astype(F32) + fixed).astype(BF16)

    parts = [(dz, p) for p in range(3) for dz in range(2)]
    for dz, p in parts:
        for dc, ab in mates:
            result(dz, p, dc, ab).wait_recv()
    for copy in sends:
        copy.wait_send()
    for k in range(4):
        pass_on(k).wait_send()
        for i in range(3):
            stat_copy(k, i).wait_send()
    for p in range(3):
        for q in range(3):
            for k in range(4):
                stage(p, q, k).wait_send()
    for p in range(3):
        for k in range(4):
            for way in range(2):
                hop(p, k, way).wait_send()
    for dz in range(2):
        for k in range(4):
            y_send(dz, k).wait_send()
            core_send(dz, k).wait_send()
    for i in range(3):
        x_send(i).wait_send()
        left_send(i).wait_send()
        swap(i).wait_send()
    left_core.wait_send()
    for dz, p in parts:
        for dc, ab in mates:
            result(dz, p, dc, ab).wait_send()
    pltpu.make_async_copy(res.at[:, :, 0, 0], got.at[:, :, 0, 0], osem).wait()


def deliver_kernel(got, outputs, block_grad, out, grad_out, tgrad, egrad, mgrad, sgrad, sem):
    r, m, x, y, z, c = place()
    grads = named(tgrad, egrad, mgrad, sgrad)
    out[...] = outputs[...]
    grad_out[...] = block_grad[...]

    def step(w, carry):
        dz, dc, ab = w // 8, (w // 4) % 2, w % 4
        fourth, usual, last = share_columns(*owner_of(y, z, c, ab // 2, ab % 2, dz, dc))

        def start(blocks):
            for j in range(6):
                name, index = blocks[j]
                pltpu.make_async_copy(
                    got.at[dz, j // 2, dc, ab, :, pl.ds(128 * (j % 2), 128)], grads[name].at[:, lanes(index)], sem
                ).start()

        @pl.when(fourth)
        def _():
            start(last)

        @pl.when(jnp.logical_not(fourth))
        def _():
            start(usual)

        return carry

    lax.fori_loop(0, 16, step, 0)
    pltpu.make_async_copy(got, got, sem).wait()


def params(number=None):
    if number is None:
        return pltpu.CompilerParams(vmem_limit_bytes=VMEM_LIMIT)
    return pltpu.CompilerParams(collective_id=number, has_side_effects=True, vmem_limit_bytes=VMEM_LIMIT)


VM = pl.BlockSpec(memory_space=pltpu.VMEM)
HB = pl.BlockSpec(memory_space=pl.ANY)
SEM = pltpu.SemaphoreType.DMA


def shape(*dims, dtype=BF16):
    return jax.ShapeDtypeStruct(dims, dtype)


def block(inp, cot, tri, exp, mer, shr):
    return pl.pallas_call(
        block_kernel,
        out_shape=(shape(64, 384), shape(64, 384), shape(2, 3, 2, 4, 96, 256)),
        in_specs=[VM, VM, HB, HB, HB, HB],
        out_specs=(VM, VM, HB),
        scratch_shapes=[
            pltpu.VMEM((3, 16, 384, 256), BF16),
            pltpu.VMEM((3, 3, 2, 8, 96, 256), BF16),
            pltpu.VMEM((3, 3, 8, 96, 256), BF16),
            pltpu.VMEM((3, 3, 4, 96, 256), BF16),
            pltpu.VMEM((3, 3, 2, 96, 256), BF16),
            pltpu.VMEM((3, 3, 1, 96, 256), BF16),
            pltpu.VMEM((4, 64, 128), F32),
            pltpu.VMEM((4, 3, 64, 128), F32),
            pltpu.VMEM((64, 384), BF16),
            pltpu.VMEM((2, 256, 384), BF16),
            pltpu.VMEM((4, 96, 128), BF16),
            pltpu.VMEM((4, 96, 128), BF16),
            pltpu.VMEM((4, 4, 96, 128), BF16),
            pltpu.VMEM((64, 384), F32),
            pltpu.VMEM((3, 256, 256), F32),
            pltpu.VMEM((3, 256, 256), BF16),
            pltpu.VMEM((2, 4, 2, 3, 256, 256), BF16),
            pltpu.VMEM((2, 256, 384), F32),
            pltpu.VMEM((2, 256, 384), BF16),
            pltpu.VMEM((3, 2, 64, 384), BF16),
            pltpu.VMEM((8, 3, 256, 256), BF16),
            pltpu.VMEM((2, 2, 4, 4, 96, 256), BF16),
            pltpu.VMEM((2, 3, 2, 4, 96, 256), BF16),
            SEM((3,)), SEM((3, 3)), SEM((3, 3)), SEM((4, 3)), SEM((4, 3)), SEM((3, 3, 4)), SEM((3, 3, 4)),
            SEM((3,)), SEM((3,)), SEM((4,)), SEM((4,)),
            SEM((3, 4, 2)), SEM((3, 4, 2)), SEM((2, 4)), SEM((2, 4)), SEM((2, 4)), SEM((2, 4)),
            SEM((4,)), SEM((4,)), SEM((2, 3, 2, 4)), SEM((2, 3, 2, 4)), SEM(()),
        ],
        compiler_params=params(0),
        name="block",
    )(inp, cot, tri, exp, mer, shr)


def deliver(got, outputs, block_grad):
    return pl.pallas_call(
        deliver_kernel,
        out_shape=(
            shape(64, 384), shape(64, 384), shape(3, 96, 1536), shape(96, 3072), shape(96, 1536), shape(96, 3072),
        ),
        in_specs=[VM] * 3,
        out_specs=(VM, VM) + (HB,) * 4,
        scratch_shapes=[SEM(())],
        compiler_params=params(),
        name="deliver",
    )(got, outputs, block_grad)


def body(inputs, triple_weight, expand_weight, merge_weight, shrink_weight, cotangent):
    weights = (triple_weight.transpose(1, 0, 2), expand_weight, merge_weight, shrink_weight)
    outputs, block_grad, got = block(inputs, cotangent, *weights)
    outputs, block_grad, tg, eg, mg, sg = deliver(got, outputs, block_grad)
    return outputs, block_grad, tg.transpose(1, 0, 2), eg, mg, sg


def solution(mesh):
    placed = (
        P(("dp", "my"), "mx"),
        P("mx", None, "my"),
        P("mx", "my"),
        P("mx", "my"),
        P("mx", "my"),
        P(("dp", "my"), "mx"),
    )
    return jax.shard_map(
        body,
        mesh=mesh,
        in_specs=placed,
        out_specs=(
            P(("dp", "my"), "mx"),
            P(("dp", "my"), "mx"),
            P(("mx", "dp"), None, "my"),
            P(("mx", "dp"), "my"),
            P(("mx", "dp"), "my"),
            P(("mx", "dp"), "my"),
        ),
        check_vma=False,
    )
```

time: 139 us -> 121 us (0.87); the launches traced: 137 us -> 121 us
  Pallas kernels: 129 us -> 120 us
  local copies, waits for them, and re-layouts: 7.44 us -> 0 us
    pallas_call x3 -> x2, Pallas kernels: 129 us -> 120 us  [the longest x1 116 us: block(): pl.pallas_call(block_kernel, out_shape=(shape(64, 384), shape(64, 384), s...]
    unnamed x12 -> x0, local copies, waits for them, and re-layouts: 7.44 us -> none
where the time goes in v3:
time: 121 us
  Pallas kernels  120 us (99%)
    pallas_call x1, Pallas kernels, block(): pl.pallas_call(block_kernel, out_shape=(shape(64, 384), shape(64, 384), s...  116 us
    pallas_call x1, Pallas kernels, deliver(): pl.pallas_call(deliver_kernel, out_shape=(shape(64, 384), shape(64, 384),...  3.97 us

profile of v3, /device:TPU:1, one launch (start us, length us, event | category | flops | bytes accessed | tf_op | source)
XLA Modules:
  0.0 121.1 jit_solution(8803212988879505309)
XLA Ops:
  0.6 116.3 %block.1 = (bf16[64,384]{1,0:T(8,128)(2,1)}, bf16[64,384]{1,0:T(8,128)(2,1)}, bf16[2,3,2,4,96,256]{5,4,3,2,1,0:T(8,128)(2,1)}) custom-call(bf16[64,384]{1,0:T(8,128)(2,1)} %inp.1, bf16[64,384]{1,0:T(8,128)(2,1)} %cot.1, bf16[3,384,1536]{2,1,0:T(8,128)(2,1)} %bitcast.2, bf16[384,3072]{1,0:T(8,128)(2,1)} %exp.1, bf16[384,1536]{1,0:T(8,128)(2,1)} %mer.1, ...), custom_call_target="tpu_custom_call" | custom-call | tf_op jit(solution)/shard_map/block/pallas_call | solution.py:650
  116.9 4.0 %deliver.1 = (bf16[64,384]{1,0:T(8,128)(2,1)}, bf16[64,384]{1,0:T(8,128)(2,1)}, bf16[3,96,1536]{2,1,0:T(8,128)(2,1)}, bf16[96,3072]{1,0:T(8,128)(2,1)}, bf16[96,...) custom-call(bf16[2,3,2,4,96,256]{5,4,3,2,1,0:T(8,128)(2,1)} %get-tuple-element.15.got, ...), custom_call_target="tpu_custom_call" | custom-call | tf_op jit(solution)/shard_map/deliver/pallas_call | solution.py:690

commit v4 on v3

--- a/solution.py
+++ b/solution.py
@@ -19,6 +19,7 @@
 VMEM_LIMIT = 60 * 1024 * 1024
 
 SEQ = ((0, 1, 2), (1, 2, 0), (2, 0, 1))
+PAIRS = ((0, 2), (1, 3), (4, 5))
 CUTS = (((0, 96), (96, 80), (176, 80)), ((0, 80), (80, 96), (176, 80)), ((0, 80), (80, 80), (160, 96)))
 
 
@@ -44,9 +45,9 @@
     k = zo * 2 + co
     head = 3 * yo + k
     unit = 6 * yo + k
-    usual = (("m", head), ("s", unit), ("q", head), ("k", head), ("v", head), ("e", unit))
+    usual = (("s", unit), ("m", head), ("e", unit), ("q", head), ("k", head), ("v", head))
     first = 6 * yo + 3
-    fourth = (("s", first), ("s", first + 1), ("s", first + 2), ("e", first), ("e", first + 1), ("e", first + 2))
+    fourth = (("s", first), ("s", first + 1), ("e", first), ("s", first + 2), ("e", first + 1), ("e", first + 2))
     return k == 3, usual, fourth
 
 
@@ -125,44 +126,41 @@
     return pre * phi, phi + pre * jnp.exp(-0.5 * pre * pre) * INV_ROOT_TAU
 
 
+LEFT = slice(0, 128)
+RIGHT = slice(128, 256)
+
+
+def hidden_unit(proj, out, pre_at, grad_at, value_to, slope_to):
+    value, slope = gelu_pair(proj[pre_at[0], :, pre_at[1]])
+    grad = proj[grad_at[0], :, grad_at[1]]
+    out[value_to[0], :, value_to[1]] = value.astype(BF16)
+    out[slope_to[0], :, slope_to[1]] = (grad * slope).astype(BF16)
+
+
 def middle(proj, out, fourth):
-    def left(p):
-        return (p, slice(None), slice(0, 128))
-
-    def right(p):
-        return (p, slice(None), slice(128, 256))
-
-    def unit(pre_at, grad_at):
-        value, slope = gelu_pair(proj[pre_at])
-        grad = proj[grad_at]
-        out[grad_at] = value.astype(BF16)
-        out[pre_at] = (grad * slope).astype(BF16)
-
     @pl.when(fourth)
     def _():
-        unit(right(1), left(0))
-        unit(left(2), right(0))
-        unit(right(2), left(1))
+        hidden_unit(proj, out, (2, LEFT), (0, RIGHT), (1, LEFT), (2, LEFT))
+        hidden_unit(proj, out, (2, RIGHT), (1, RIGHT), (1, RIGHT), (2, RIGHT))
 
     @pl.when(jnp.logical_not(fourth))
     def _():
-        unit(right(2), right(0))
-        qhat, qinv = norm_heads(proj[left(1)])
-        khat, kinv = norm_heads(proj[right(1)])
+        qhat, qinv = norm_heads(proj[1, :, RIGHT])
+        khat, kinv = norm_heads(proj[2, :, LEFT])
         q, k = qhat.astype(BF16), khat.astype(BF16)
-        v = proj[left(2)].astype(BF16)
-        datt = proj[left(0)].astype(BF16)
+        v = proj[2, :, RIGHT].astype(BF16)
+        datt = proj[0, :, RIGHT].astype(BF16)
         expo = jnp.exp(dot_last(q, k) * SCALE)
         probs = expo / jnp.sum(expo, axis=-1, keepdims=True)
         half = probs.astype(BF16)
-        out[left(0)] = jnp.dot(half, v, preferred_element_type=F32).astype(BF16)
+        out[1, :, LEFT] = jnp.dot(half, v, preferred_element_type=F32).astype(BF16)
         g = dot_last(datt, v)
         ds = (probs * (g - jnp.sum(probs * g, axis=-1, keepdims=True))).astype(BF16)
         dqn = jnp.dot(ds, k, preferred_element_type=F32) * SCALE
         dkn = dot_first(ds, q) * SCALE
-        out[left(1)] = norm_backward(dqn, qhat, qinv).astype(BF16)
-        out[right(1)] = norm_backward(dkn, khat, kinv).astype(BF16)
-        out[left(2)] = dot_first(half, datt).astype(BF16)
+        out[1, :, RIGHT] = norm_backward(dqn, qhat, qinv).astype(BF16)
+        out[2, :, LEFT] = norm_backward(dkn, khat, kinv).astype(BF16)
+        out[2, :, RIGHT] = dot_first(half, datt).astype(BF16)
 
 
 def block_kernel(
@@ -256,8 +254,8 @@
 
             if p == 1:
                 fourth = ((z + dz) % 2) * ((c + dc) % 2)
-                first = jnp.dot(both[fourth], held[p, s, :, 0:128], preferred_element_type=F32)
-                second = jnp.dot(both[0], held[p, s, :, 128:256], preferred_element_type=F32)
+                first = jnp.dot(both[0], held[p, s, :, 0:128], preferred_element_type=F32)
+                second = jnp.dot(both[fourth], held[p, s, :, 128:256], preferred_element_type=F32)
                 put(first.astype(BF16), slice(0, 128))
                 put(second.astype(BF16), slice(128, 256))
             else:
@@ -315,6 +313,121 @@
         if k == 2:
             return remote(spread.at[0:2, 2], spread.at[0:2, 3], *sem, {"mx": peers[1]})
         return remote(spread.at[2:4, 1], spread.at[2:4, 3], *sem, {"mx": peers[0]})
+
+    top, bottom = pl.ds(0, 128), pl.ds(128, 128)
+
+    def hop(p, k, way):
+        sem = (zs.at[p, k, way], zr.at[p, k, way])
+        if way == 0:
+            src = down.at[p] if k == 0 else ring.at[8 - k, p]
+            dst = ring.at[7 - k, p]
+            if k == 3:
+                src, dst = src.at[top], dst.at[top]
+            return remote(src, dst, *sem, up)
+        src = down.at[p] if k == 0 else ring.at[k, p]
+        dst = ring.at[k + 1, p]
+        if k == 3:
+            src, dst = src.at[bottom], dst.at[bottom]
+        return remote(src, dst, *sem, below)
+
+    def hop_start(p, k):
+        hop(p, k, 0).start()
+        hop(p, k, 1).start()
+
+    def hop_wait(p, k):
+        hop(p, k, 0).wait_recv()
+        hop(p, k, 1).wait_recv()
+
+    def share(p, dz):
+        return down.at[p] if dz == 0 else ring.at[1 + 6 * z, p]
+
+    def y_send(p, dz, k):
+        sem = (ys.at[p, dz, k], yr.at[p, dz, k])
+        if k == 0:
+            return remote(share(p, dz), slots.at[dz, 2, 0, p], *sem, {"mx": peers[0]})
+        if k == 1:
+            return remote(share(p, dz), slots.at[dz, 1, 0, p], *sem, {"mx": peers[1]})
+        if k == 2:
+            return remote(slots.at[dz, 2, 0, p, top], slots.at[dz, 3, 0, p, top], *sem, {"mx": peers[1]})
+        return remote(slots.at[dz, 1, 0, p, bottom], slots.at[dz, 3, 0, p, bottom], *sem, {"mx": peers[0]})
+
+    def core_send(p, dz, ab):
+        src = slots.at[dz, ab, 0, p] if ab else share(p, dz)
+        return remote(src, slots.at[dz, ab, 1, p], cs.at[p, dz, ab], cr.at[p, dz, ab], {"mx": peers[3]})
+
+    def spread_share(p, dz):
+        y_send(p, dz, 0).start()
+        y_send(p, dz, 1).start()
+        core_send(p, dz, 0).start()
+
+    def pass_share(p, dz):
+        y_send(p, dz, 0).wait_recv()
+        y_send(p, dz, 2).start()
+        core_send(p, dz, 2).start()
+        y_send(p, dz, 1).wait_recv()
+        y_send(p, dz, 3).start()
+        core_send(p, dz, 1).start()
+
+    def last_share(p, dz):
+        y_send(p, dz, 2).wait_recv()
+        y_send(p, dz, 3).wait_recv()
+        core_send(p, dz, 3).start()
+
+    def left_at(q):
+        return left.at[q // 2, 0, :, :, :, lanes(q % 2)]
+
+    def left_send(i):
+        return remote(spread, left_at(x), ls.at[i], lr.at[i], {"my": xpeers[i]})
+
+    left_core = remote(left.at[:, 0], left.at[:, 1], ls.at[3], lr.at[3], {"mx": peers[3]})
+
+    def dgrad(data, dz, ab, dc):
+        s = ab * 4 + dz * 2 + dc
+        fourth = ((z + dz) % 2) * ((c + dc) % 2)
+        values = jnp.concatenate([data[0, :, LEFT], data[1, :, LEFT]], axis=1)
+        acc[0] += dot_last(values, held[0, s])
+        acc[1] += dot_last(data[0, :, RIGHT], held[1, s, :, LEFT]) + dot_last(data[2], held[2, s])
+        acc[1 - fourth] += dot_last(data[1, :, RIGHT], held[1, s, :, RIGHT])
+
+    def use(dz, ab):
+        dgrad(slots.at[dz, ab, 0], dz, ab, 0)
+
+    def use_other(dz, ab):
+        for p in range(3):
+            core_send(p, dz, ab).wait_recv()
+        dgrad(slots.at[dz, ab, 1], dz, ab, 1)
+
+    def result(dz, p, dc, ab):
+        return remote(
+            res.at[dz, p, dc, ab], got.at[dz, p, dc, ab], gs.at[dz, p, dc, ab], gr.at[dz, p, dc, ab], mate(dc, ab)
+        )
+
+    def weight_part(dz, p):
+        fourth = ((z + dz) % 2) * c
+
+        def total(dc, side, columns):
+            sum_of = None
+            for k in range(4):
+                d = (dz * (1 + 6 * z) + 2 * k) % 8
+                term = jnp.dot(
+                    left[side, dc, k].reshape(384, 256), ring[d, p, :, columns], preferred_element_type=F32
+                )
+                sum_of = term if sum_of is None else sum_of + term
+            return sum_of.astype(BF16).reshape(4, 96, -1)
+
+        for dc in range(2):
+            if p < 2:
+                res[dz, p, dc, :, :, LEFT] = total(dc, 1, LEFT)
+                res[dz, p, dc, :, :, RIGHT] = total(dc, fourth if p else 0, RIGHT)
+            else:
+                res[dz, p, dc] = total(dc, 0, slice(0, 256))
+        pltpu.make_async_copy(res.at[dz, p, 0, 0], got.at[dz, p, 0, 0], osem).start()
+        for dc, ab in mates:
+            result(dz, p, dc, ab).start()
+
+    def x_send(i):
+        rows_of = pl.ds(pl.multiple_of(xpeers[i] * 64, 64), 64)
+        return remote(xsend.at[:, rows_of], xgot.at[i], xs.at[2, i], xr.at[2, i], {"my": xpeers[i]})
 
     gathered(0)
     wait_weights(0, held, wsem)
@@ -341,9 +454,10 @@
     begin(1)
     multiply(1, 0)
     wait_weights(2, held, wsem)
+    advance(1, 0)
     multiply(2, 1)
     begin(2)
-    advance(1, 0)
+    advance(0, 2)
 
     quarter = both[x // 2, pl.ds(pl.multiple_of((x % 2) * 128, 128), 128), :]
     turned[...] = quarter.T.reshape(4, 96, 128)
@@ -351,192 +465,91 @@
         swap(i).start()
     mixed[0] = turned[r]
     multiply(2, 0)
+    advance(1, 1)
     advance(2, 0)
-    advance(0, 2)
-    advance(1, 1)
-    advance(2, 1)
+    advance(1, 2)
+    advance(0, 3)
     for i in range(3):
         swap(i).wait_recv()
     pass_on(0).start()
     pass_on(1).start()
     spread[:, 0] = mixed[...]
-    advance(1, 2)
-    advance(2, 2)
+    advance(2, 1)
+    advance(1, 3)
+
+    hidden_unit(proj, down, (1, LEFT), (0, LEFT), (0, LEFT), (0, RIGHT))
+    hop_start(0, 0)
+    spread_share(0, 0)
+    ring[0, 0] = down[0]
     pass_on(0).wait_recv()
     pass_on(2).start()
     pass_on(1).wait_recv()
     pass_on(3).start()
-    for p in range(3):
-        advance(p, 3)
-    middle(proj, down, z * 2 + c == 3)
-
-    top, bottom = pl.ds(0, 128), pl.ds(128, 128)
-
-    def hop(p, k, way):
-        sem = (zs.at[p, k, way], zr.at[p, k, way])
-        if way == 0:
-            src = down.at[p] if k == 0 else ring.at[8 - k, p]
-            dst = ring.at[7 - k, p]
-            if k == 3:
-                src, dst = src.at[top], dst.at[top]
-            return remote(src, dst, *sem, up)
-        src = down.at[p] if k == 0 else ring.at[k, p]
-        dst = ring.at[k + 1, p]
-        if k == 3:
-            src, dst = src.at[bottom], dst.at[bottom]
-        return remote(src, dst, *sem, below)
-
-    def hop_start(p, k):
-        hop(p, k, 0).start()
-        hop(p, k, 1).start()
-
-    def hop_wait(p, k):
-        hop(p, k, 0).wait_recv()
-        hop(p, k, 1).wait_recv()
-
-    def y_send(dz, k):
-        src = down if dz == 0 else ring.at[1 + 6 * z]
-        sem = (ys.at[dz, k], yr.at[dz, k])
-        if k == 0:
-            return remote(src, slots.at[dz, 2, 0], *sem, {"mx": peers[0]})
-        if k == 1:
-            return remote(src, slots.at[dz, 1, 0], *sem, {"mx": peers[1]})
-        if k == 2:
-            return remote(slots.at[dz, 2, 0, :, top], slots.at[dz, 3, 0, :, top], *sem, {"mx": peers[1]})
-        return remote(slots.at[dz, 1, 0, :, bottom], slots.at[dz, 3, 0, :, bottom], *sem, {"mx": peers[0]})
-
-    def core_send(dz, ab):
-        src = slots.at[dz, ab, 0]
-        if ab == 0:
-            src = down if dz == 0 else ring.at[1 + 6 * z]
-        return remote(src, slots.at[dz, ab, 1], cs.at[dz, ab], cr.at[dz, ab], {"mx": peers[3]})
-
-    def left_at(q):
-        return left.at[q // 2, 0, :, :, :, lanes(q % 2)]
-
-    def left_send(i):
-        return remote(spread, left_at(x), ls.at[i], lr.at[i], {"my": xpeers[i]})
-
-    left_core = remote(left.at[:, 0], left.at[:, 1], ls.at[3], lr.at[3], {"mx": peers[3]})
-
-    for p in range(3):
-        hop_start(p, 0)
-    y_send(0, 0).start()
-    y_send(0, 1).start()
-    core_send(0, 0).start()
+    advance(2, 2)
+    acc[...] = jnp.zeros_like(acc)
+    hop_wait(0, 0)
+    hop_start(0, 1)
+    spread_share(0, 1)
     pass_on(2).wait_recv()
     pass_on(3).wait_recv()
     for i in range(3):
         left_send(i).start()
     left[x // 2, 0, :, :, :, lanes(x % 2)] = spread[...]
-    ring[0] = down[...]
-    acc[...] = jnp.zeros_like(acc)
-
-    def dgrad(data, dz, ab, dc):
-        s = ab * 4 + dz * 2 + dc
-        fourth = ((z + dz) % 2) * ((c + dc) % 2)
-        acc[0] += dot_last(data[0], held[0, s])
-        acc[1] += dot_last(data[1, :, 128:256], held[1, s, :, 128:256]) + dot_last(data[2], held[2, s])
-        acc[1 - fourth] += dot_last(data[1, :, 0:128], held[1, s, :, 0:128])
-
-    def use(dz, ab):
-        dgrad(slots.at[dz, ab, 0], dz, ab, 0)
-
-    def use_other(dz, ab):
-        core_send(dz, ab).wait_recv()
-        dgrad(slots.at[dz, ab, 1], dz, ab, 1)
-
-    def result(dz, p, dc, ab):
-        return remote(
-            res.at[dz, p, dc, ab], got.at[dz, p, dc, ab], gs.at[dz, p, dc, ab], gr.at[dz, p, dc, ab], mate(dc, ab)
-        )
-
-    def weight_part(dz, p):
-        fourth = ((z + dz) % 2) * c
-
-        def total(dc, side, columns):
-            sum_of = None
-            for k in range(4):
-                d = (dz * (1 + 6 * z) + 2 * k) % 8
-                term = jnp.dot(
-                    left[side, dc, k].reshape(384, 256), ring[d, p, :, columns], preferred_element_type=F32
-                )
-                sum_of = term if sum_of is None else sum_of + term
-            return sum_of.astype(BF16).reshape(4, 96, -1)
-
-        for dc in range(2):
-            if p == 1:
-                res[dz, p, dc, :, :, 0:128] = total(dc, fourth, slice(0, 128))
-                res[dz, p, dc, :, :, 128:256] = total(dc, 0, slice(128, 256))
-            else:
-                res[dz, p, dc] = total(dc, 1 if p == 0 else 0, slice(0, 256))
-        pltpu.make_async_copy(res.at[dz, p, 0, 0], got.at[dz, p, 0, 0], osem).start()
-        for dc, ab in mates:
-            result(dz, p, dc, ab).start()
-
-    def x_send(i):
-        rows_of = pl.ds(pl.multiple_of(xpeers[i] * 64, 64), 64)
-        return remote(xsend.at[:, rows_of], xgot.at[i], xs.at[2, i], xr.at[2, i], {"my": xpeers[i]})
-
+    advance(2, 3)
+    pass_share(0, 0)
+    middle(proj, down, z * 2 + c == 3)
+
+    for p in (1, 2):
+        hop_start(p, 0)
+    for p in (1, 2):
+        spread_share(p, 0)
+    ring[0, 1:3] = down[1:3]
+    hop_wait(0, 1)
+    hop_start(0, 2)
     dgrad(down, 0, 0, 0)
-    hop_wait(0, 0)
-    hop_start(0, 1)
-    hop_wait(1, 0)
-    hop_start(1, 1)
-    hop_wait(2, 0)
-    y_send(1, 0).start()
-    y_send(1, 1).start()
-    core_send(1, 0).start()
-    y_send(0, 0).wait_recv()
-    y_send(0, 2).start()
-    core_send(0, 2).start()
-    y_send(0, 1).wait_recv()
-    y_send(0, 3).start()
-    core_send(0, 1).start()
+    pass_share(0, 1)
+    last_share(0, 0)
+    for p in (1, 2):
+        hop_wait(p, 0)
+        hop_start(p, 1)
+        spread_share(p, 1)
+    hop_wait(0, 2)
+    hop_start(0, 3)
     use_other(0, 0)
     dgrad(ring.at[1 + 6 * z], 1, 0, 0)
-    hop_wait(0, 1)
-    hop_start(0, 2)
-    hop_wait(1, 1)
-    hop_start(1, 2)
+    for p in (1, 2):
+        pass_share(p, 0)
     use(0, 2)
     use(0, 1)
+    for i in range(3):
+        remote(spread, left_at((x + 3 - i) % 4), ls.at[i], lr.at[i], {"my": xpeers[i]}).wait_recv()
+    left_core.start()
+    for p in (1, 2):
+        hop_wait(p, 1)
+        hop_start(p, 2)
+    last_share(0, 1)
+    hop_wait(0, 3)
     use_other(1, 0)
-    hop_wait(0, 2)
-    hop_start(0, 3)
-    hop_wait(1, 2)
-    hop_start(1, 3)
-    hop_start(2, 1)
-    y_send(0, 2).wait_recv()
-    y_send(0, 3).wait_recv()
-    core_send(0, 3).start()
-    y_send(1, 0).wait_recv()
-    y_send(1, 2).start()
-    core_send(1, 2).start()
-    y_send(1, 1).wait_recv()
-    y_send(1, 3).start()
-    core_send(1, 1).start()
-    for i in range(3):
-        rows_of = left_at((x + 3 - i) % 4)
-        remote(spread, rows_of, ls.at[i], lr.at[i], {"my": xpeers[i]}).wait_recv()
-    left_core.start()
+    left_core.wait_recv()
+    weight_part(0, 0)
+    weight_part(1, 0)
+    for p in (1, 2):
+        pass_share(p, 1)
+        last_share(p, 0)
+    for p in (1, 2):
+        hop_wait(p, 2)
+        hop_start(p, 3)
     use(0, 3)
     use_other(0, 2)
     use_other(0, 1)
-    hop_wait(2, 1)
-    hop_start(2, 2)
-    hop_wait(0, 3)
-    left_core.wait_recv()
-    weight_part(0, 0)
-    weight_part(1, 0)
     hop_wait(1, 3)
-    hop_wait(2, 2)
-    hop_start(2, 3)
     weight_part(0, 1)
     weight_part(1, 1)
-    y_send(1, 2).wait_recv()
-    y_send(1, 3).wait_recv()
-    core_send(1, 3).start()
+    hop_wait(2, 3)
+    weight_part(0, 2)
+    weight_part(1, 2)
+    for p in (1, 2):
+        last_share(p, 1)
     use(1, 2)
     use(1, 1)
     use(1, 3)
@@ -547,9 +560,6 @@
     xsend[...] = acc[...].astype(BF16)
     for i in range(3):
         x_send(i).start()
-    hop_wait(2, 3)
-    weight_part(0, 2)
-    weight_part(1, 2)
     own = pl.ds(pl.multiple_of(x * 64, 64), 64)
     branch = acc[0, own, :]
     grad = acc[1, own, :]
@@ -585,10 +595,9 @@
         for k in range(4):
             for way in range(2):
                 hop(p, k, way).wait_send()
-    for dz in range(2):
-        for k in range(4):
-            y_send(dz, k).wait_send()
-            core_send(dz, k).wait_send()
+            for dz in range(2):
+                y_send(p, dz, k).wait_send()
+                core_send(p, dz, k).wait_send()
     for i in range(3):
         x_send(i).wait_send()
         left_send(i).wait_send()
@@ -612,7 +621,7 @@
 
         def start(blocks):
             for j in range(6):
-                name, index = blocks[j]
+                name, index = blocks[PAIRS[j // 2][j % 2]]
                 pltpu.make_async_copy(
                     got.at[dz, j // 2, dc, ab, :, pl.ds(128 * (j % 2), 128)], grads[name].at[:, lanes(index)], sem
                 ).start()
@@ -678,7 +687,7 @@
             pltpu.VMEM((2, 3, 2, 4, 96, 256), BF16),
             SEM((3,)), SEM((3, 3)), SEM((3, 3)), SEM((4, 3)), SEM((4, 3)), SEM((3, 3, 4)), SEM((3, 3, 4)),
             SEM((3,)), SEM((3,)), SEM((4,)), SEM((4,)),
-            SEM((3, 4, 2)), SEM((3, 4, 2)), SEM((2, 4)), SEM((2, 4)), SEM((2, 4)), SEM((2, 4)),
+            SEM((3, 4, 2)), SEM((3, 4, 2)), SEM((3, 2, 4)), SEM((3, 2, 4)), SEM((3, 2, 4)), SEM((3, 2, 4)),
             SEM((4,)), SEM((4,)), SEM((2, 3, 2, 4)), SEM((2, 3, 2, 4)), SEM(()),
         ],
         compiler_params=params(0),

time: 121 us -> 119 us (0.983)
  Pallas kernels: 120 us -> 118 us
    pallas_call x1, Pallas kernels: 116 us -> 114 us  [block(): pl.pallas_call(block_kernel, out_shape=(shape(64, 384), shape(64, 384), s...]
where the time goes in v4:
time: 119 us
  Pallas kernels  118 us (99%)
    pallas_call x1, Pallas kernels, block(): pl.pallas_call(block_kernel, out_shape=(shape(64, 384), shape(64, 384), s...  114 us
    pallas_call x1, Pallas kernels, deliver(): pl.pallas_call(deliver_kernel, out_shape=(shape(64, 384), shape(64, 384),...  3.97 us

profile of v4, /device:TPU:1, one launch (start us, length us, event | category | flops | bytes accessed | tf_op | source)
XLA Modules:
  0.0 119.0 jit_solution(9238554400973048319)
XLA Ops:
  0.6 114.2 %block.1 = (bf16[64,384]{1,0:T(8,128)(2,1)}, bf16[64,384]{1,0:T(8,128)(2,1)}, bf16[2,3,2,4,96,256]{5,4,3,2,1,0:T(8,128)(2,1)}) custom-call(bf16[64,384]{1,0:T(8,128)(2,1)} %inp.1, bf16[64,384]{1,0:T(8,128)(2,1)} %cot.1, bf16[3,384,1536]{2,1,0:T(8,128)(2,1)} %bitcast.2, bf16[384,3072]{1,0:T(8,128)(2,1)} %exp.1, bf16[384,1536]{1,0:T(8,128)(2,1)} %mer.1, ...), custom_call_target="tpu_custom_call" | custom-call | tf_op jit(solution)/shard_map/block/pallas_call | solution.py:659
  114.8 4.0 %deliver.1 = (bf16[64,384]{1,0:T(8,128)(2,1)}, bf16[64,384]{1,0:T(8,128)(2,1)}, bf16[3,96,1536]{2,1,0:T(8,128)(2,1)}, bf16[96,3072]{1,0:T(8,128)(2,1)}, bf16[96,...) custom-call(bf16[2,3,2,4,96,256]{5,4,3,2,1,0:T(8,128)(2,1)} %get-tuple-element.15.got, ...), custom_call_target="tpu_custom_call" | custom-call | tf_op jit(solution)/shard_map/deliver/pallas_call | solution.py:699

commit v5 on v4

--- a/solution.py
+++ b/solution.py
@@ -165,9 +165,10 @@
 
 def block_kernel(
     inp, cot, tri, exp, mer, shr, outputs, block_grad, got,
-    held, part, got0, got1, got2, got3, stat_out, stat_in, nown, both, turned, mixed, spread, hat, proj, down,
+    held, part, got0, got1, got2, got3, stat_out, stat_in, row_stats, local, stat_near, stat_all, col_sums, sums_near,
+    sums_all, stat_cols, nown, both, turned, mixed, spread, hat, proj, down,
     slots, acc, xsend, xgot, ring, left, res,
-    wsem, xs, xr, ss, sr, rs, rr, es, er, fs, fr, zs, zr, ys, yr, cs, cr, ls, lr, gs, gr, osem,
+    wsem, xs, xr, ss, sr, ns, nr, rs, rr, es, er, fs, fr, zs, zr, ys, yr, cs, cr, ls, lr, gs, gr, osem,
 ):
     r, m, x, y, z, c = place()
     refs = named(tri, exp, mer, shr)
@@ -190,24 +191,40 @@
         ({"mx": peers[3]}, {"mx": peers[2]}, {"mx": peers[2] + other_core}),
         ({"mx": peers[0]}, {"mx": peers[1]}, {"mx": opposite}),
     )
-    greet(
-        [{"my": q} for q in xpeers] + [{"dp": q} for q in rpeers] + [up, below, rounds[0][2]]
-        + [mate(dc, ab) for dc, ab in mates]
-    )
-
-    own = pl.ds(pl.multiple_of(x * 64, 64), 64)
-    sends = []
-    for i in range(3):
-        copy = remote(cot, both.at[1, own], xs.at[0, i], xr.at[0, i], {"my": xpeers[i]})
-        copy.start()
-        sends.append(copy)
-    both[1, own, :] = cot[...]
+    load_weights(0, refs, held, wsem, y, z, c)
 
     rows = inp[...].astype(F32)
     mean = jnp.sum(rows, axis=1, keepdims=True) / rows.shape[1]
     centred = rows - mean
     square = jnp.sum(centred * centred, axis=1, keepdims=True)
     low = lax.broadcasted_iota(jnp.int32, (64, 128), 1) < 64
+    nown[0] = centred.astype(BF16)
+    local[...] = jnp.where(low, mean, square)
+    greet(
+        [{"my": q} for q in xpeers] + [{"dp": q} for q in rpeers] + [up, below, rounds[0][2]]
+        + [mate(dc, ab) for dc, ab in mates]
+    )
+
+    own = pl.ds(pl.multiple_of(x * 64, 64), 64)
+    sends = []
+
+    def to_rows(k, src, full):
+        for i in range(3):
+            copy = remote(src, full.at[own], xs.at[k, i], xr.at[k, i], {"my": xpeers[i]})
+            copy.start()
+            sends.append(copy)
+        full[own, :] = src[...]
+
+    def gathered(k, full):
+        for i in range(3):
+            rows_of = full.at[pl.ds(pl.multiple_of(((x + 3 - i) % 4) * 64, 64), 64)]
+            remote(rows_of, rows_of, xs.at[k, i], xr.at[k, i], {"my": xpeers[i]}).wait_recv()
+
+    to_rows(0, cot, both.at[1])
+    to_rows(1, nown.at[0], both.at[0])
+    to_rows(3, local, row_stats)
+    both[0, 256:272, :] = jnp.ones((16, 384), BF16)
+    col_sums[...] = jnp.zeros_like(col_sums)
 
     def stat_copy(k, i):
         return remote(stat_out.at[k], stat_in.at[k, i], ss.at[k, i], sr.at[k, i], rounds[k % 2][i])
@@ -216,6 +233,24 @@
         stat_out[k] = jnp.where(low, pair[0], pair[1])
         for i in range(3):
             stat_copy(k, i).start()
+
+    def near_copy(k, i):
+        ab = (2, 1, 3)[i]
+        src, dst = (
+            (stat_near.at[0], stat_near.at[i + 1]),
+            (stat_near, stat_all.at[ab]),
+            (col_sums.at[i + 1], sums_near.at[i + 1]),
+            (sums_near.at[:, ab], sums_all.at[ab]),
+        )[k]
+        return remote(src, dst, ns.at[k, i], nr.at[k, i], rounds[k % 2][i])
+
+    def near_start(k):
+        for i in range(3):
+            near_copy(k, i).start()
+
+    def near_finish(k):
+        for i in range(3):
+            near_copy(k, i).wait_recv()
 
     def stat_finish(k):
         pairs = []
@@ -223,23 +258,6 @@
             stat_copy(k, i).wait_recv()
             pairs.append((stat_in[k, i, :, 0:1], stat_in[k, i, :, 64:65]))
         return pairs
-
-    def combine(own_pair, pairs, count):
-        pairs = [own_pair] + pairs
-        middle_of = sum(pair[0] for pair in pairs) / 4
-        spread_of = sum(pair[1] + count * (pair[0] - middle_of) ** 2 for pair in pairs)
-        return middle_of, spread_of
-
-    pair = (mean, square)
-    stat_start(0, pair)
-    load_weights(0, refs, held, wsem, y, z, c)
-    pair = combine(pair, stat_finish(0), 384.0)
-    stat_start(1, pair)
-
-    def gathered(k):
-        for i in range(3):
-            rows_of = both.at[1 - k, pl.ds(pl.multiple_of(((x + 3 - i) % 4) * 64, 64), 64)]
-            remote(rows_of, rows_of, xs.at[k, i], xr.at[k, i], {"my": xpeers[i]}).wait_recv()
 
     def multiply(p, dc):
         def step(t, carry):
@@ -252,18 +270,21 @@
                     at, size = CUTS[p][q]
                     part[p, q, dc, places[q], 0:size, columns] = value[at : at + size]
 
+            if p == 0:
+                put(jnp.dot(both[1, 0:256], held[p, s], preferred_element_type=F32).astype(BF16), slice(0, 256))
+            else:
+                value = jnp.dot(both[0], held[p, s], preferred_element_type=F32)
+                put(value[0:256].astype(BF16), slice(0, 256))
+                col_sums[dc + 2 * dz, da * 2 + db, p : p + 1] = value[256:257]
             if p == 1:
-                fourth = ((z + dz) % 2) * ((c + dc) % 2)
-                first = jnp.dot(both[0], held[p, s, :, 0:128], preferred_element_type=F32)
-                second = jnp.dot(both[fourth], held[p, s, :, 128:256], preferred_element_type=F32)
-                put(first.astype(BF16), slice(0, 128))
-                put(second.astype(BF16), slice(128, 256))
-            else:
-                full = both[1 if p == 0 else 0]
-                put(jnp.dot(full, held[p, s], preferred_element_type=F32).astype(BF16), slice(0, 256))
+
+                @pl.when(((z + dz) % 2) * ((c + dc) % 2) == 1)
+                def _():
+                    put(jnp.dot(both[1, 0:256], held[p, s, :, RIGHT], preferred_element_type=F32).astype(BF16), RIGHT)
+
             return carry
 
-        lax.fori_loop(0, 8, step, 0)
+        lax.fori_loop(0, 8, step, 0, unroll=4)
 
     def stage(p, q, k):
         size = CUTS[p][q][1]
@@ -293,26 +314,71 @@
                 return carry
 
             if k < 3:
-                lax.fori_loop(0, 8 >> k, step, 0)
+                lax.fori_loop(0, 8 >> k, step, 0, unroll=2)
                 stage(p, q, k + 1).start()
             else:
                 proj[p, at : at + size] = (
                     part[p, q, 0, 0, 0:size].astype(F32) + source[p, q, 0, 0:size].astype(F32)
                 )
 
-    def swap(i):
+    half, piece = x % 2, pl.ds(pl.multiple_of((x // 2) * 48, 48), 48)
+
+    def turn(side, full):
+        quarter = full[pl.ds(pl.multiple_of(half * 128, 128), 128), :]
+        turned[side] = quarter.T.reshape(4, 96, 128)
+        for i in range(3):
+            swap(side, i).start()
+        mixed[side, 0] = turned[side, r, piece]
+
+    def swap(side, i):
         q = rpeers[i]
-        return remote(turned.at[q], mixed.at[3 - i], es.at[i], er.at[i], {"dp": q})
-
-    def pass_on(k):
-        sem = (fs.at[k], fr.at[k])
+        return remote(turned.at[side, q, piece], mixed.at[side, 3 - i], es.at[side, i], er.at[side, i], {"dp": q})
+
+    def pass_on(side, k):
+        sem = (fs.at[side, k], fr.at[side, k])
         if k == 0:
-            return remote(mixed, spread.at[:, 2], *sem, {"mx": peers[0]})
+            return remote(mixed.at[side], spread.at[side, :, 2], *sem, {"mx": peers[0]})
         if k == 1:
-            return remote(mixed, spread.at[:, 1], *sem, {"mx": peers[1]})
+            return remote(mixed.at[side], spread.at[side, :, 1], *sem, {"mx": peers[1]})
         if k == 2:
-            return remote(spread.at[0:2, 2], spread.at[0:2, 3], *sem, {"mx": peers[1]})
-        return remote(spread.at[2:4, 1], spread.at[2:4, 3], *sem, {"mx": peers[0]})
+            return remote(spread.at[side, 0:2, 2], spread.at[side, 0:2, 3], *sem, {"mx": peers[1]})
+        return remote(spread.at[side, 2:4, 1], spread.at[side, 2:4, 3], *sem, {"mx": peers[0]})
+
+    def pass_first(side):
+        for i in range(3):
+            swap(side, i).wait_recv()
+        pass_on(side, 0).start()
+        pass_on(side, 1).start()
+        spread[side, :, 0] = mixed[side]
+
+    def pass_second(side):
+        pass_on(side, 0).wait_recv()
+        pass_on(side, 2).start()
+        pass_on(side, 1).wait_recv()
+        pass_on(side, 3).start()
+
+    def left_at(side, q):
+        rows_of = pl.ds(pl.multiple_of((q // 2) * 48, 48), 48)
+        return left.at[side, 0, :, :, rows_of, lanes(q % 2)]
+
+    def left_send(side, i):
+        return remote(spread.at[side], left_at(side, x), ls.at[side, i], lr.at[side, i], {"my": xpeers[i]})
+
+    def left_core(side):
+        return remote(left.at[side, 0], left.at[side, 1], ls.at[side, 3], lr.at[side, 3], {"mx": peers[3]})
+
+    def pass_third(side):
+        pass_on(side, 2).wait_recv()
+        pass_on(side, 3).wait_recv()
+        for i in range(3):
+            left_send(side, i).start()
+        left[side, 0, :, :, piece, lanes(half)] = spread[side]
+
+    def left_here(side):
+        for i in range(3):
+            q = (x + 3 - i) % 4
+            remote(spread.at[side], left_at(side, q), ls.at[side, i], lr.at[side, i], {"my": xpeers[i]}).wait_recv()
+        left_core(side).start()
 
     top, bottom = pl.ds(0, 128), pl.ds(128, 128)
 
@@ -373,14 +439,6 @@
         y_send(p, dz, 3).wait_recv()
         core_send(p, dz, 3).start()
 
-    def left_at(q):
-        return left.at[q // 2, 0, :, :, :, lanes(q % 2)]
-
-    def left_send(i):
-        return remote(spread, left_at(x), ls.at[i], lr.at[i], {"my": xpeers[i]})
-
-    left_core = remote(left.at[:, 0], left.at[:, 1], ls.at[3], lr.at[3], {"mx": peers[3]})
-
     def dgrad(data, dz, ab, dc):
         s = ab * 4 + dz * 2 + dc
         fourth = ((z + dz) % 2) * ((c + dc) % 2)
@@ -429,75 +487,101 @@
         rows_of = pl.ds(pl.multiple_of(xpeers[i] * 64, 64), 64)
         return remote(xsend.at[:, rows_of], xgot.at[i], xs.at[2, i], xr.at[2, i], {"my": xpeers[i]})
 
-    gathered(0)
+    def settle(p):
+        sub = lax.broadcasted_iota(jnp.int32, (128, 256), 0) % 8
+        moved = jnp.where(sub == p, stat_all[...].reshape(128, 256) - row_mean, 0.0)
+        shift = lax.dot_general(
+            moved, sums_all[...].reshape(128, 256), (((0,), (0,)), ((), ())),
+            precision=lax.Precision.HIGHEST, preferred_element_type=F32,
+        )
+        scaled = (proj[p] + shift) * stat_cols[:, 1:2]
+        if p == 1:
+            keep = jnp.logical_and(
+                z * 2 + c == 3, lax.broadcasted_iota(jnp.int32, (256, 256), 1) >= 128
+            )
+            scaled = jnp.where(keep, proj[p], scaled)
+        proj[p] = scaled
+
+    load_weights(1, refs, held, wsem, y, z, c)
+    gathered(0, both.at[1])
     wait_weights(0, held, wsem)
     multiply(0, 1)
     begin(0)
-    pair = combine(pair, stat_finish(1), 1536.0)
-    inverse = lax.rsqrt(pair[1] / WIDTH + EPS)
-    unit = (rows - pair[0]) * inverse
-    nown[...] = unit.astype(BF16)
-    both[0, own, :] = unit.astype(BF16)
-    for i in range(3):
-        copy = remote(nown, both.at[0, own], xs.at[1, i], xr.at[1, i], {"my": xpeers[i]})
-        copy.start()
-        sends.append(copy)
-    hat[...] = unit
-    multiply(0, 0)
-    load_weights(1, refs, held, wsem, y, z, c)
-    advance(0, 0)
+    turn(1, both.at[1])
     load_weights(2, refs, held, wsem, y, z, c)
-    advance(0, 1)
-    gathered(1)
+    gathered(3, row_stats)
+    across = row_stats[...].T
+    stat_near[0] = jnp.where(lax.broadcasted_iota(jnp.int32, (8, 256), 0) < 4, across[0:8], across[64:72])
+    near_start(0)
+    gathered(1, both.at[0])
     wait_weights(1, held, wsem)
     multiply(1, 1)
     begin(1)
+    multiply(0, 0)
+    advance(0, 0)
+    pass_first(1)
     multiply(1, 0)
+    near_finish(0)
+    near_start(1)
     wait_weights(2, held, wsem)
-    advance(1, 0)
     multiply(2, 1)
     begin(2)
+    pass_second(1)
+    advance(1, 0)
+    multiply(2, 0)
+    sums_near[0] = col_sums[0]
+    near_start(2)
+    advance(0, 1)
+    advance(2, 0)
+
+    stat_all[0] = stat_near[...]
+    near_finish(1)
+    sub = lax.broadcasted_iota(jnp.int32, (128, 256), 0) % 8
+    every = stat_all[...].reshape(128, 256)
+    row_mean = jnp.sum(jnp.where(sub == 0, every, 0.0), axis=0, keepdims=True) / 16
+    apart = jnp.where(sub == 0, every - row_mean, 0.0)
+    row_square = jnp.sum(jnp.where(sub == 4, every, 0.0) + 384.0 * apart * apart, axis=0, keepdims=True)
+    row_inverse = lax.rsqrt(row_square / WIDTH + EPS)
+    first_row = lax.broadcasted_iota(jnp.int32, (128, 256), 0) == 0
+    stat_cols[...] = jnp.where(first_row, row_mean, row_inverse).T
+    inverse = stat_cols[own, 1:2]
+    unit = (rows - stat_cols[own, 0:1]) * inverse
+    hat[...] = unit
+    nown[1] = unit.astype(BF16)
+    to_rows(4, nown.at[1], both.at[2])
+    near_finish(2)
+    near_start(3)
+    advance(1, 1)
     advance(0, 2)
-
-    quarter = both[x // 2, pl.ds(pl.multiple_of((x % 2) * 128, 128), 128), :]
-    turned[...] = quarter.T.reshape(4, 96, 128)
-    for i in range(3):
-        swap(i).start()
-    mixed[0] = turned[r]
-    multiply(2, 0)
-    advance(1, 1)
-    advance(2, 0)
+    gathered(4, both.at[2])
+
+    turn(0, both.at[2])
+    pass_third(1)
+    advance(2, 1)
     advance(1, 2)
     advance(0, 3)
-    for i in range(3):
-        swap(i).wait_recv()
-    pass_on(0).start()
-    pass_on(1).start()
-    spread[:, 0] = mixed[...]
-    advance(2, 1)
+    pass_first(0)
+    sums_all[0] = sums_near[:, 0]
+    near_finish(3)
     advance(1, 3)
+    settle(1)
 
     hidden_unit(proj, down, (1, LEFT), (0, LEFT), (0, LEFT), (0, RIGHT))
     hop_start(0, 0)
     spread_share(0, 0)
     ring[0, 0] = down[0]
-    pass_on(0).wait_recv()
-    pass_on(2).start()
-    pass_on(1).wait_recv()
-    pass_on(3).start()
+    pass_second(0)
     advance(2, 2)
     acc[...] = jnp.zeros_like(acc)
+    advance(2, 3)
+    settle(2)
+    pass_third(0)
+    middle(proj, down, z * 2 + c == 3)
+    left_here(1)
     hop_wait(0, 0)
     hop_start(0, 1)
     spread_share(0, 1)
-    pass_on(2).wait_recv()
-    pass_on(3).wait_recv()
-    for i in range(3):
-        left_send(i).start()
-    left[x // 2, 0, :, :, :, lanes(x % 2)] = spread[...]
-    advance(2, 3)
     pass_share(0, 0)
-    middle(proj, down, z * 2 + c == 3)
 
     for p in (1, 2):
         hop_start(p, 0)
@@ -506,52 +590,56 @@
     ring[0, 1:3] = down[1:3]
     hop_wait(0, 1)
     hop_start(0, 2)
-    dgrad(down, 0, 0, 0)
     pass_share(0, 1)
     last_share(0, 0)
-    for p in (1, 2):
-        hop_wait(p, 0)
-        hop_start(p, 1)
-        spread_share(p, 1)
+    hop_wait(1, 0)
+    hop_start(1, 1)
+    spread_share(1, 1)
+    hop_wait(2, 0)
+    spread_share(2, 1)
+    dgrad(down, 0, 0, 0)
     hop_wait(0, 2)
     hop_start(0, 3)
-    use_other(0, 0)
-    dgrad(ring.at[1 + 6 * z], 1, 0, 0)
+    left_here(0)
     for p in (1, 2):
         pass_share(p, 0)
+    hop_wait(1, 1)
+    hop_start(1, 2)
+    hop_start(2, 1)
+    last_share(0, 1)
+    use_other(0, 0)
+    hop_wait(0, 3)
+    for side in range(2):
+        left_core(side).wait_recv()
+    for p in (1, 2):
+        pass_share(p, 1)
+    weight_part(0, 0)
+    weight_part(1, 0)
+    hop_wait(1, 2)
+    hop_start(1, 3)
+    hop_wait(2, 1)
+    hop_start(2, 2)
+    for p in (1, 2):
+        last_share(p, 0)
+    dgrad(ring.at[1 + 6 * z], 1, 0, 0)
     use(0, 2)
     use(0, 1)
-    for i in range(3):
-        remote(spread, left_at((x + 3 - i) % 4), ls.at[i], lr.at[i], {"my": xpeers[i]}).wait_recv()
-    left_core.start()
+    hop_wait(1, 3)
+    weight_part(0, 1)
+    weight_part(1, 1)
+    hop_wait(2, 2)
+    hop_start(2, 3)
     for p in (1, 2):
-        hop_wait(p, 1)
-        hop_start(p, 2)
-    last_share(0, 1)
-    hop_wait(0, 3)
+        last_share(p, 1)
     use_other(1, 0)
-    left_core.wait_recv()
-    weight_part(0, 0)
-    weight_part(1, 0)
-    for p in (1, 2):
-        pass_share(p, 1)
-        last_share(p, 0)
-    for p in (1, 2):
-        hop_wait(p, 2)
-        hop_start(p, 3)
     use(0, 3)
     use_other(0, 2)
     use_other(0, 1)
-    hop_wait(1, 3)
-    weight_part(0, 1)
-    weight_part(1, 1)
+    use(1, 2)
+    use(1, 1)
     hop_wait(2, 3)
     weight_part(0, 2)
     weight_part(1, 2)
-    for p in (1, 2):
-        last_share(p, 1)
-    use(1, 2)
-    use(1, 1)
     use(1, 3)
     use_other(0, 3)
     for ab in (2, 1, 3):
@@ -584,9 +672,12 @@
     for copy in sends:
         copy.wait_send()
     for k in range(4):
-        pass_on(k).wait_send()
-        for i in range(3):
-            stat_copy(k, i).wait_send()
+        for side in range(2):
+            pass_on(side, k).wait_send()
+        for i in range(3):
+            near_copy(k, i).wait_send()
+            if k > 1:
+                stat_copy(k, i).wait_send()
     for p in range(3):
         for q in range(3):
             for k in range(4):
@@ -600,9 +691,11 @@
                 core_send(p, dz, k).wait_send()
     for i in range(3):
         x_send(i).wait_send()
-        left_send(i).wait_send()
-        swap(i).wait_send()
-    left_core.wait_send()
+        for side in range(2):
+            left_send(side, i).wait_send()
+            swap(side, i).wait_send()
+    for side in range(2):
+        left_core(side).wait_send()
     for dz, p in parts:
         for dc, ab in mates:
             result(dz, p, dc, ab).wait_send()
@@ -670,11 +763,19 @@
             pltpu.VMEM((3, 3, 1, 96, 256), BF16),
             pltpu.VMEM((4, 64, 128), F32),
             pltpu.VMEM((4, 3, 64, 128), F32),
-            pltpu.VMEM((64, 384), BF16),
-            pltpu.VMEM((2, 256, 384), BF16),
-            pltpu.VMEM((4, 96, 128), BF16),
-            pltpu.VMEM((4, 96, 128), BF16),
-            pltpu.VMEM((4, 4, 96, 128), BF16),
+            pltpu.VMEM((256, 128), F32),
+            pltpu.VMEM((64, 128), F32),
+            pltpu.VMEM((4, 8, 256), F32),
+            pltpu.VMEM((4, 4, 8, 256), F32),
+            pltpu.VMEM((4, 4, 8, 256), F32),
+            pltpu.VMEM((4, 4, 8, 256), F32),
+            pltpu.VMEM((4, 4, 8, 256), F32),
+            pltpu.VMEM((256, 128), F32),
+            pltpu.VMEM((2, 64, 384), BF16),
+            pltpu.VMEM((3, 272, 384), BF16),
+            pltpu.VMEM((2, 4, 96, 128), BF16),
+            pltpu.VMEM((2, 4, 48, 128), BF16),
+            pltpu.VMEM((2, 4, 4, 48, 128), BF16),
             pltpu.VMEM((64, 384), F32),
             pltpu.VMEM((3, 256, 256), F32),
             pltpu.VMEM((3, 256, 256), BF16),
@@ -685,10 +786,10 @@
             pltpu.VMEM((8, 3, 256, 256), BF16),
             pltpu.VMEM((2, 2, 4, 4, 96, 256), BF16),
             pltpu.VMEM((2, 3, 2, 4, 96, 256), BF16),
-            SEM((3,)), SEM((3, 3)), SEM((3, 3)), SEM((4, 3)), SEM((4, 3)), SEM((3, 3, 4)), SEM((3, 3, 4)),
-            SEM((3,)), SEM((3,)), SEM((4,)), SEM((4,)),
+            SEM((3,)), SEM((5, 3)), SEM((5, 3)), SEM((4, 3)), SEM((4, 3)), SEM((4, 3)), SEM((4, 3)), SEM((3, 3, 4)), SEM((3, 3, 4)),
+            SEM((2, 3)), SEM((2, 3)), SEM((2, 4)), SEM((2, 4)),
             SEM((3, 4, 2)), SEM((3, 4, 2)), SEM((3, 2, 4)), SEM((3, 2, 4)), SEM((3, 2, 4)), SEM((3, 2, 4)),
-            SEM((4,)), SEM((4,)), SEM((2, 3, 2, 4)), SEM((2, 3, 2, 4)), SEM(()),
+            SEM((2, 4)), SEM((2, 4)), SEM((2, 3, 2, 4)), SEM((2, 3, 2, 4)), SEM(()),
         ],
         compiler_params=params(0),
         name="block",

time: 119 us -> 115 us (0.966)
  Pallas kernels: 118 us -> 114 us
    pallas_call x1, Pallas kernels: 114 us -> 110 us  [block(): pl.pallas_call(block_kernel, out_shape=(shape(64, 384), shape(64, 384), s...]
where the time goes in v5:
time: 115 us
  Pallas kernels  114 us (99%)
    pallas_call x1, Pallas kernels, block(): pl.pallas_call(block_kernel, out_shape=(shape(64, 384), shape(64, 384), s...  110 us
    pallas_call x1, Pallas kernels, deliver(): pl.pallas_call(deliver_kernel, out_shape=(shape(64, 384), shape(64, 384),...  3.97 us

profile of v5, /device:TPU:1, one launch (start us, length us, event | category | flops | bytes accessed | tf_op | source)
XLA Modules:
  0.0 115.1 jit_solution(13675419337892547731)
XLA Ops:
  0.6 110.3 %block.1 = (bf16[64,384]{1,0:T(8,128)(2,1)}, bf16[64,384]{1,0:T(8,128)(2,1)}, bf16[2,3,2,4,96,256]{5,4,3,2,1,0:T(8,128)(2,1)}) custom-call(bf16[64,384]{1,0:T(8,128)(2,1)} %inp.1, bf16[64,384]{1,0:T(8,128)(2,1)} %cot.1, bf16[3,384,1536]{2,1,0:T(8,128)(2,1)} %bitcast.2, bf16[384,3072]{1,0:T(8,128)(2,1)} %exp.1, bf16[384,1536]{1,0:T(8,128)(2,1)} %mer.1, ...), custom_call_target="tpu_custom_call" | custom-call | tf_op jit(solution)/shard_map/block/pallas_call | solution.py:752
  111.0 4.0 %deliver.1 = (bf16[64,384]{1,0:T(8,128)(2,1)}, bf16[64,384]{1,0:T(8,128)(2,1)}, bf16[3,96,1536]{2,1,0:T(8,128)(2,1)}, bf16[96,3072]{1,0:T(8,128)(2,1)}, bf16[96,...) custom-call(bf16[2,3,2,4,96,256]{5,4,3,2,1,0:T(8,128)(2,1)} %get-tuple-element.15.got, ...), custom_call_target="tpu_custom_call" | custom-call | tf_op jit(solution)/shard_map/deliver/pallas_call | solution.py:800

commit v6 on v5

--- a/solution.py
+++ b/solution.py
@@ -637,9 +637,6 @@
     use_other(0, 1)
     use(1, 2)
     use(1, 1)
-    hop_wait(2, 3)
-    weight_part(0, 2)
-    weight_part(1, 2)
     use(1, 3)
     use_other(0, 3)
     for ab in (2, 1, 3):
@@ -648,6 +645,9 @@
     xsend[...] = acc[...].astype(BF16)
     for i in range(3):
         x_send(i).start()
+    hop_wait(2, 3)
+    weight_part(0, 2)
+    weight_part(1, 2)
     own = pl.ds(pl.multiple_of(x * 64, 64), 64)
     branch = acc[0, own, :]
     grad = acc[1, own, :]

time: 115 us -> 115 us (level)
  no operation moved by 1% of the time
where the time goes in v6:
time: 115 us
  Pallas kernels  114 us (99%)
    pallas_call x1, Pallas kernels, block(): pl.pallas_call(block_kernel, out_shape=(shape(64, 384), shape(64, 384), s...  110 us
    pallas_call x1, Pallas kernels, deliver(): pl.pallas_call(deliver_kernel, out_shape=(shape(64, 384), shape(64, 384),...  3.97 us

profile of v6, /device:TPU:1, one launch (start us, length us, event | category | flops | bytes accessed | tf_op | source)
XLA Modules:
  0.0 115.1 jit_solution(1300023532816473257)
XLA Ops:
  0.6 110.3 %block.1 = (bf16[64,384]{1,0:T(8,128)(2,1)}, bf16[64,384]{1,0:T(8,128)(2,1)}, bf16[2,3,2,4,96,256]{5,4,3,2,1,0:T(8,128)(2,1)}) custom-call(bf16[64,384]{1,0:T(8,128)(2,1)} %inp.1, bf16[64,384]{1,0:T(8,128)(2,1)} %cot.1, bf16[3,384,1536]{2,1,0:T(8,128)(2,1)} %bitcast.2, bf16[384,3072]{1,0:T(8,128)(2,1)} %exp.1, bf16[384,1536]{1,0:T(8,128)(2,1)} %mer.1, ...), custom_call_target="tpu_custom_call" | custom-call | tf_op jit(solution)/shard_map/block/pallas_call | solution.py:752
  111.0 4.0 %deliver.1 = (bf16[64,384]{1,0:T(8,128)(2,1)}, bf16[64,384]{1,0:T(8,128)(2,1)}, bf16[3,96,1536]{2,1,0:T(8,128)(2,1)}, bf16[96,3072]{1,0:T(8,128)(2,1)}, bf16[96,...) custom-call(bf16[2,3,2,4,96,256]{5,4,3,2,1,0:T(8,128)(2,1)} %get-tuple-element.15.got, ...), custom_call_target="tpu_custom_call" | custom-call | tf_op jit(solution)/shard_map/deliver/pallas_call | solution.py:800
